TPU v7x, 32 devices: a whole 2x2x4 slice. The times are simulated.
32 devices in a mesh: group: 2 (over x), blk: 16 (over z, y, core).
Axes of the slice: x: 2, y: 2, z: 4, core: 2. Of those that a mesh axis runs over, the one named last changes fastest.
Arguments:
- stack_wet_layers: int32 [128, 32, 128], P(('group', 'blk')), parts along dimension 0, may hold values from 0 to 20, as said below
- patch_owner: int32 [128], P('group'), parts along dimension 0, may hold values from 0 to 15, as said below
- piece_owner: int32 [512], P('group'), parts along dimension 0, may hold values from -1 to 15, as said below
- piece_neighbours: int32 [512, 8], P('group'), parts along dimension 0, may hold values from 0 to 256, as said below
- east_velocity: float32 [128, 20, 32, 128], P(('group', 'blk')), parts along dimension 0, may hold values from -6 to 6
- north_velocity: float32 [128, 20, 32, 128], P(('group', 'blk')), parts along dimension 0, may hold values from -6 to 6
- heat_anomaly: float32 [128, 20, 32, 128], P(('group', 'blk')), parts along dimension 0, may hold values from -6 to 6
- saltiness_anomaly: float32 [128, 20, 32, 128], P(('group', 'blk')), parts along dimension 0, may hold values from -6 to 6
- diffusivity_below: float32 [128, 20, 32, 128], P(('group', 'blk')), parts along dimension 0, may hold values from 0.05 to 20
Outputs:
- east_velocity_next: float32 [128, 20, 32, 128], P(('group', 'blk')), parts along dimension 0
- north_velocity_next: float32 [128, 20, 32, 128], P(('group', 'blk')), parts along dimension 0
- heat_anomaly_mixed: float32 [128, 20, 32, 128], P(('group', 'blk')), parts along dimension 0
- saltiness_mixed: float32 [128, 20, 32, 128], P(('group', 'blk')), parts along dimension 0
- sea_height_patches: float32 [448, 8, 128], P(('group', 'blk')), parts along dimension 0
There are 2 independent parts, one for each index of `group`. A program takes and returns all parts, laid end to end along the dimension named above; each array names one. Nothing has to cross between parts.
Inputs may be any that keep to these rules, and one draw needn't show every extreme that they name: `stack_wet_layers`: ocean levels of each column; 0 on land; every column of a tile whose piece_owner is -1 is land. `patch_owner`: each device of blk owns exactly 4 blocks, a run of consecutive block numbers. `piece_owner`: -1 marks a tile left out of the solve; every device owns exactly 14 tiles; of the tiles of the blocks of one device at most 2 have the same owner, exactly 2 for some pair of devices. `piece_neighbours`: row t lists the tiles above, below, left of, right of, above-left, above-right, below-left and below-right of tile t, 256 where there is none or where that tile's owner is -1.
All inputs are finite; a program needn't handle non-finite values.
Results may differ from a plain program's by a relative error of at most 0.0003.
Values sent between devices are 32-bit elements; how exact they have to be, the bound alone decides.
A program may use at most 64 MiB of HBM per device.

v0:
```python
import jax
import jax.numpy as jnp
from jax import lax
from jax.sharding import PartitionSpec as P

BLK_DEV = 4
SPLIT = 4
BT_DEV = 14
ITERS = 6
SUB = 4
TILES_DEV = 16


NEIGHBOR_SIDES = (
    (-1, 0, 1.0),
    (1, 0, 1.0),
    (0, -1, 1.0),
    (0, 1, 1.0),
    (-1, -1, 0.25),
    (-1, 1, 0.25),
    (1, -1, 0.25),
    (1, 1, 0.25),
)
damping = 0.1
coriolis = 0.3
lowest = 0.02
highest = 2.0


def level_steps(count):
    return 1.0 + 0.1 * jnp.arange(count).astype(jnp.float32)


def stack_mixer(field, barotropic_linkage, iteration_number):
    levels = field.shape[1]
    zeros = jnp.zeros_like(field[:, 0])
    ratio = zeros
    value = zeros
    ratios = []
    values = []
    for level in range(levels):
        lower = barotropic_linkage[:, level - 1] if level > 0 else zeros
        upper = barotropic_linkage[:, level]
        denom = iteration_number[level] + lower + upper - lower * ratio
        value = (iteration_number[level] * field[:, level] + lower * value) / denom
        ratio = upper / denom
        ratios.append(ratio)
        values.append(value)
    current = values[levels - 1]
    result = [current]
    for level in range(levels - 2, -1, -1):
        current = values[level] + ratios[level] * current
        result.append(current)
    return jnp.stack(result[::-1], axis=1)


def internal_wave_part(
    stack_wet_layers,
    east_velocity,
    north_velocity,
    heat_anomaly,
    saltiness_anomaly,
    diffusivity_below,
):
    count = east_velocity.shape[1]
    iteration_number = level_steps(count)
    water_indicator = (jnp.arange(count)[None, :, None, None] < stack_wet_layers[:, None]).astype(
        jnp.float32
    )
    below = jnp.concatenate(
        [water_indicator[:, 1:], jnp.zeros_like(water_indicator[:, :1])], axis=1
    )
    barotropic_linkage = diffusivity_below * below
    zonal_pred = water_indicator * (east_velocity + coriolis * north_velocity)
    meridional_pred = water_indicator * (north_velocity - coriolis * east_velocity)
    east_velocity_mixed = stack_mixer(zonal_pred, barotropic_linkage, iteration_number)
    north_velocity_mixed = stack_mixer(meridional_pred, barotropic_linkage, iteration_number)
    heat_anomaly_mixed = water_indicator * stack_mixer(
        heat_anomaly, 0.5 * barotropic_linkage, iteration_number
    )
    saltiness_mixed = water_indicator * stack_mixer(
        saltiness_anomaly, 0.5 * barotropic_linkage, iteration_number
    )
    total = jnp.sum(iteration_number)
    weights = iteration_number[None, :, None, None]
    transport_east = jnp.sum(weights * east_velocity_mixed, axis=1) / total
    transport_north = jnp.sum(weights * north_velocity_mixed, axis=1) / total
    layer_thickness_share = jnp.sum(weights * water_indicator, axis=1) / total
    return (
        water_indicator,
        east_velocity_mixed,
        north_velocity_mixed,
        heat_anomaly_mixed,
        saltiness_mixed,
        transport_east,
        transport_north,
        layer_thickness_share,
    )


def to_tiles(field):
    count = field.shape[0]
    rows = field.shape[1] // SPLIT
    return field.reshape(count * SPLIT, rows, field.shape[2])


def from_tiles(tiles, count):
    return tiles.reshape(count, SPLIT * tiles.shape[1], tiles.shape[2])


def rim_of(field, width):
    count = field.shape[0]
    return jnp.concatenate(
        [
            field[:, :width, :].reshape(count, -1),
            field[:, field.shape[1] - width :, :].reshape(count, -1),
            field[:, :, :width].reshape(count, -1),
            field[:, :, field.shape[2] - width :].reshape(count, -1),
        ],
        axis=1,
    )


def assemble(own, rims, width):
    count, rows, cols = own.shape
    edge = width * cols
    side = rows * width

    def top_of(which):
        return rims[:, which, :edge].reshape(count, width, cols)

    def bottom_of(which):
        return rims[:, which, edge : 2 * edge].reshape(count, width, cols)

    upper = jnp.concatenate(
        [bottom_of(4)[:, :, cols - width :], bottom_of(0), bottom_of(5)[:, :, :width]], axis=2
    )
    middle = jnp.concatenate(
        [
            rims[:, 2, 2 * edge + side :].reshape(count, rows, width),
            own,
            rims[:, 3, 2 * edge : 2 * edge + side].reshape(count, rows, width),
        ],
        axis=2,
    )
    lower = jnp.concatenate(
        [top_of(6)[:, :, cols - width :], top_of(1), top_of(7)[:, :, :width]], axis=2
    )
    return jnp.concatenate([upper, middle, lower], axis=1)


def shifted(field, down, across):
    rows = field.shape[1]
    cols = field.shape[2]
    padded = jnp.pad(field, ((0, 0), (1, 1), (1, 1)))
    return padded[:, 1 + down : 1 + down + rows, 1 + across : 1 + across + cols]


def crop(field, width):
    return field[:, width : field.shape[1] - width, width : field.shape[2] - width]


def couplings(depth_pad):
    ocean = (depth_pad > 0).astype(jnp.float32)
    weights = []
    diagonal = damping + jnp.zeros_like(depth_pad)
    for down, across, factor in NEIGHBOR_SIDES:
        weight = (
            factor
            * 0.5
            * (depth_pad + shifted(depth_pad, down, across))
            * ocean
            * shifted(ocean, down, across)
        )
        weights.append(weight)
        diagonal = diagonal + weight
    return (weights, diagonal, ocean)


def apply_operator(field, weights, diagonal):
    result = diagonal * field
    for (down, across, factor), weight in zip(NEIGHBOR_SIDES, weights):
        result = result - weight * shifted(field, down, across)
    return result


def chebyshev_plan(count):
    centre = 0.5 * (highest + lowest)
    spread = 0.5 * (highest - lowest)
    sigma = centre / spread
    rho = 1.0 / sigma
    plan = []
    for step in range(count):
        fresh = 1.0 / (2.0 * sigma - rho)
        plan.append((fresh * rho, 2.0 * fresh / spread))
        rho = fresh
    return (centre, plan)


def group_rank(owner):
    total = owner.shape[0]
    order = jnp.argsort(owner, stable=True)
    ordered = owner[order]
    first = jnp.searchsorted(ordered, ordered, side="left")
    positions = jnp.arange(total) - first
    return jnp.zeros((total,), jnp.int32).at[order].set(positions)


def earlier_matrix(count):
    places = jnp.arange(count, dtype=jnp.int32)
    return places[None, :] < places[:, None]


def pick_rows(gathered, index):
    padded = jnp.concatenate([gathered, jnp.zeros((1, gathered.shape[1]), gathered.dtype)], axis=0)
    return padded[index]


def pack_slots(tiles, slots, total):
    return jnp.zeros((total,) + tiles.shape[1:], tiles.dtype).at[slots].set(tiles, mode="drop")


def barotropic(zonal_tiles, north_tiles, depth_tiles, tile_ids, locate, piece_neighbours, sentinel):
    locate_all = jnp.concatenate([locate, jnp.full((1,), sentinel, jnp.int32)])
    index = locate_all[piece_neighbours[tile_ids]]
    rows = zonal_tiles.shape[1]
    cols = zonal_tiles.shape[2]
    width = 1
    got_zonal, got_north, got_depth = (
        lax.all_gather(rim_of(zonal_tiles, width), "blk", axis=0, tiled=True),
        lax.all_gather(rim_of(north_tiles, width), "blk", axis=0, tiled=True),
        lax.all_gather(rim_of(depth_tiles, width), "blk", axis=0, tiled=True),
    )
    zonal_pad = assemble(zonal_tiles, pick_rows(got_zonal, index), width)
    north_pad = assemble(north_tiles, pick_rows(got_north, index), width)
    depth_pad = assemble(depth_tiles, pick_rows(got_depth, index), width)
    weights, diagonal, ocean = couplings(depth_pad)
    ocean_mid = crop(ocean, width)
    diagonal_mid = crop(diagonal, width)
    rhs = (
        -(
            crop(zonal_pad, width)
            - zonal_pad[:, width : width + rows, width - 1 : width - 1 + cols]
            + crop(north_pad, width)
            - north_pad[:, width - 1 : width - 1 + rows, width : width + cols]
        )
        * ocean_mid
    )
    centre, plan = chebyshev_plan(ITERS)
    height = jnp.zeros_like(rhs)
    resid = rhs
    search = resid / (centre * diagonal_mid)
    for start in range(0, ITERS, width):
        got_search = lax.all_gather(rim_of(search, 1), "blk", axis=0, tiled=True)
        search_pad = assemble(search, pick_rows(got_search, index), 1)
        resid_pad = jnp.pad(resid, ((0, 0), (1, 1), (1, 1)))
        height = height + crop(search_pad, width)
        resid_pad = resid_pad - apply_operator(search_pad, weights, diagonal)
        if start + 1 < ITERS:
            first, second = plan[start]
            search_pad = first * search_pad + second * resid_pad / diagonal
        search = crop(search_pad, width)
        resid = crop(resid_pad, width)
    got_height = lax.all_gather(rim_of(height, 1), "blk", axis=0, tiled=True)
    height_pad = assemble(height, pick_rows(got_height, index), 1)
    ocean_one = crop(ocean, width - 1)
    ocean_core = crop(ocean_one, 1)
    east = (height_pad[:, 1:-1, 2:] - height) * ocean_core * ocean_one[:, 1:-1, 2:]
    south = (height_pad[:, 2:, 1:-1] - height) * ocean_core * ocean_one[:, 2:, 1:-1]
    return (height, east, south)


def on_device(
    stack_wet_layers,
    patch_owner,
    piece_owner,
    piece_neighbours,
    east_velocity,
    north_velocity,
    heat_anomaly,
    saltiness_anomaly,
    diffusivity_below,
):
    devices = lax.axis_size("blk")
    own_index = lax.axis_index("blk")
    capacity = max(2, TILES_DEV // devices)
    slot_total = devices * capacity
    (
        water_indicator,
        east_velocity_mixed,
        north_velocity_mixed,
        heat_anomaly_mixed,
        saltiness_mixed,
        transport_east,
        transport_north,
        layer_thickness_share,
    ) = internal_wave_part(
        stack_wet_layers,
        east_velocity,
        north_velocity,
        heat_anomaly,
        saltiness_anomaly,
        diffusivity_below,
    )
    own_blocks = jnp.nonzero(patch_owner == own_index, size=BLK_DEV)[0].astype(jnp.int32)
    own_tiles = (own_blocks[:, None] * SUB + jnp.arange(SUB, dtype=jnp.int32)[None, :]).reshape(-1)
    target = piece_owner[own_tiles]
    own_live = target >= 0
    send_rank = jnp.sum((target[:, None] == target[None, :]) & earlier_matrix(TILES_DEV), axis=1)
    send_slot = jnp.where(own_live, target * capacity + send_rank, slot_total)
    held = jnp.nonzero(piece_owner == own_index, size=BT_DEV, fill_value=0)[0].astype(jnp.int32)
    anchor = patch_owner[held // SUB]
    recv_rank = jnp.sum((anchor[:, None] == anchor[None, :]) & earlier_matrix(BT_DEV), axis=1)
    recv_slot = anchor * capacity + recv_rank
    zonal_tiles = to_tiles(transport_east)
    north_tiles = to_tiles(transport_north)
    depth_tiles = to_tiles(layer_thickness_share)
    moved_zonal, moved_north, moved_depth = (
        lax.all_to_all(
            pack_slots(zonal_tiles, send_slot, slot_total),
            "blk",
            split_axis=0,
            concat_axis=0,
            tiled=True,
        ),
        lax.all_to_all(
            pack_slots(north_tiles, send_slot, slot_total),
            "blk",
            split_axis=0,
            concat_axis=0,
            tiled=True,
        ),
        lax.all_to_all(
            pack_slots(depth_tiles, send_slot, slot_total),
            "blk",
            split_axis=0,
            concat_axis=0,
            tiled=True,
        ),
    )
    tile_rank = group_rank(piece_owner)
    locate = jnp.where(piece_owner >= 0, piece_owner * BT_DEV + tile_rank, devices * BT_DEV)
    sea_height_field, east_held, south_held = barotropic(
        moved_zonal[recv_slot],
        moved_north[recv_slot],
        moved_depth[recv_slot],
        held,
        locate,
        piece_neighbours,
        devices * BT_DEV,
    )
    got_east, got_south = (
        lax.all_to_all(
            pack_slots(east_held, recv_slot, slot_total),
            "blk",
            split_axis=0,
            concat_axis=0,
            tiled=True,
        ),
        lax.all_to_all(
            pack_slots(south_held, recv_slot, slot_total),
            "blk",
            split_axis=0,
            concat_axis=0,
            tiled=True,
        ),
    )
    keep = own_live[:, None, None]
    within = jnp.minimum(send_slot, slot_total - 1)
    east = jnp.where(keep, got_east[within], 0.0)
    south = jnp.where(keep, got_south[within], 0.0)
    east_block = from_tiles(east, BLK_DEV)
    south_block = from_tiles(south, BLK_DEV)
    east_velocity_next = water_indicator * (east_velocity_mixed - east_block[:, None])
    north_velocity_next = water_indicator * (north_velocity_mixed - south_block[:, None])
    return (
        east_velocity_next,
        north_velocity_next,
        heat_anomaly_mixed,
        saltiness_mixed,
        sea_height_field,
    )


def solution(mesh):
    placed = (
        P(("group", "blk"), None, None),
        P("group"),
        P("group"),
        P("group", None),
        P(("group", "blk"), None, None, None),
        P(("group", "blk"), None, None, None),
        P(("group", "blk"), None, None, None),
        P(("group", "blk"), None, None, None),
        P(("group", "blk"), None, None, None),
    )
    return jax.shard_map(
        on_device,
        mesh=mesh,
        in_specs=placed,
        out_specs=(
            P(("group", "blk"), None, None, None),
            P(("group", "blk"), None, None, None),
            P(("group", "blk"), None, None, None),
            P(("group", "blk"), None, None, None),
            P(("group", "blk"), None, None),
        ),
        check_vma=False,
    )
```

profile of v0, /device:TPU:0, one launch (start us, length us, event | category | flops | bytes accessed | tf_op | source)
XLA Modules:
  0.0 381.2 jit_solution(403253565731557126)
XLA Ops:
  7.6 11.1 %fusion.11 = (f32[4,1,32,128]{3,2,1,0:T(8,128)S(1)}, f32[4,1,32,128]{3,2,1,0:T(8,128)S(1)}, f32[4,1,32,128]{3,2,1,0:T(8,128)S(1)}, f32[4,1,32,128]{3,2,1,0:T(8,1...) fusion(f32[4,20,32,128]{3,2,1,0:T(8,128)S(1)} %get-tuple-elemen, ...), kind=kLoop, calls=%fused_computation.171 | loop fusion | flops 2555904 | bytes 5111880 | tf_op jit(solution)/shard_map/div | solution.py:45
  18.7 11.0 %fusion.50 = (f32[4,1,32,128]{3,2,1,0:T(8,128)S(1)}, f32[4,1,32,128]{3,2,1,0:T(8,128)S(1)}, f32[4,1,32,128]{3,2,1,0:T(8,128)S(1)}, f32[4,1,32,128]{3,2,1,0:T(8,1...) fusion(f32[4,1,32,128]{3,2,1,0:T(8,128)S(1)} %get-tuple-element, ...), kind=kLoop, calls=%fused_computation.231 | loop fusion | flops 1163264 | bytes 4522056 | tf_op jit(solution)/shard_map/div | solution.py:45
  43.0 7.4 %all-to-all-start.1 = ((f32[32,8,128]{2,1,0:T(8,128)}), f32[32,8,128]{2,1,0:T(8,128)S(1)}, u32[]{:S(2)}, u32[]{:S(2)}) async-start(f32[32,8,128]{2,1,0:T(8,128)} %scatter_fusion.1), calls=%async_computation.1 | async-start | bytes 262144 | tf_op jit(solution)/shard_map/all_to_all | solution.py:326
  54.1 3.2 sort.17
  59.3 18.4 %while.25 = (s32[]{:T(128)}, u32[256]{0:T(256)S(1)}, u32[256]{0:T(256)S(1)}, s32[256]{0:T(256)S(1)}, s32[]{:T(128)}, /*index=5*/s32[]{:T(128)}, s32[]{}) while((s32[]{:T(128)}, u32[256]{0:T(256)S(1)}, u32[256]{0:T(256)S(1)}, s32[256]{0:T(256)S(1)}, s32[]{:T(128)}, /*index=5*/s32[]{:T(128)}, s32[]{}) %tuple.321), condition=%wide.region_16.17_spmd.clone, body=%wide.region_15.16_spmd.clone.sunk | while | flops 5636 | bytes 22117 | solution.py:204
  84.7 11.2 %add_divide_fusion.8 = (f32[4,1,32,128]{3,2,1,0:T(8,128)S(1)}, f32[4,1,32,128]{3,2,1,0:T(8,128)S(1)}, f32[4,1,32,128]{3,2,1,0:T(8,128)S(1)}, f32[4,1,32,128]{3,2...) fusion(f32[4,20,32,128]{3,2,1,0:T(8,128)S(1)} %copy-done.7, ...), kind=kLoop, calls=%fused_computation.303 | loop fusion | flops 2555904 | bytes 5111880 | tf_op jit(solution)/shard_map/div | solution.py:45
  95.9 11.0 %add_divide_fusion.27 = (f32[4,1,32,128]{3,2,1,0:T(8,128)S(1)}, f32[4,1,32,128]{3,2,1,0:T(8,128)S(1)}, f32[4,1,32,128]{3,2,1,0:T(8,128)S(1)}, f32[4,1,32,128]{3,...) fusion(f32[4,1,32,128]{3,2,1,0:T(8,128)S(1)} %get-tuple-element, ...), kind=kLoop, calls=%fused_computation.342 | loop fusion | flops 1163264 | bytes 4522056 | tf_op jit(solution)/shard_map/div | solution.py:45
  119.6 6.0 %all-to-all-start = ((f32[32,8,128]{2,1,0:T(8,128)}), f32[32,8,128]{2,1,0:T(8,128)S(1)}, u32[]{:S(2)}, u32[]{:S(2)}) async-start(f32[32,8,128]{2,1,0:T(8,128)} %scatter_fusion), calls=%async_computation | async-start | bytes 262144 | tf_op jit(solution)/shard_map/all_to_all | solution.py:319
  126.7 22.8 %all-gather.1 = f32[16,14,272]{2,1,0:T(8,128)S(1)} all-gather(f32[1,14,272]{2,1,0:T(8,128)S(1)} %maximum_bitcast_fusion.1), channel_id=1, replica_groups=mesh['group'=2,'blk'=16] {'blk'}, dimensions={0}, use_global_device_ids=true | all-gather | bytes 258944 | tf_op jit(solution)/shard_map/all_gather | solution.py:231
  150.5 3.5 all-to-all-start.2
  154.7 7.2 %all-to-all-done.2 = f32[32,8,128]{2,1,0:T(8,128)S(1)} async-done(((f32[32,8,128]{2,1,0:T(8,128)}), f32[32,8,128]{2,1,0:T(8,128)S(1)}, u32[]{:S(2)}, u32[]{:S(2)}) %all-to-all-start.2) | async-done | bytes 131104 | tf_op jit(solution)/shard_map/all_to_all | solution.py:333
  163.0 19.1 %all-gather.2 = f32[16,14,272]{2,1,0:T(8,128)S(1)} all-gather(f32[1,14,272]{2,1,0:T(8,128)S(1)} %maximum_bitcast_fusion.2), channel_id=1, replica_groups=mesh['group'=2,'blk'=16] {'blk'}, dimensions={0}, use_global_device_ids=true | all-gather | bytes 258944 | tf_op jit(solution)/shard_map/all_gather | solution.py:232
  184.5 19.2 %all-gather = f32[16,14,272]{2,1,0:T(8,128)S(1)} all-gather(f32[1,14,272]{2,1,0:T(8,128)S(1)} %maximum_bitcast_fusion), channel_id=1, replica_groups=mesh['group'=2,'blk'=16] {'blk'}, dimensions={0}, use_global_device_ids=true | all-gather | bytes 258944 | tf_op jit(solution)/shard_map/all_gather | solution.py:230
  206.8 19.1 %all-gather.3 = f32[16,14,272]{2,1,0:T(8,128)S(1)} all-gather(f32[1,14,272]{2,1,0:T(8,128)S(1)} %maximum_bitcast_fusion.3), channel_id=1, replica_groups=mesh['group'=2,'blk'=16] {'blk'}, dimensions={0}, use_global_device_ids=true | all-gather | bytes 258944 | tf_op jit(solution)/shard_map/all_gather | solution.py:254
  229.6 19.5 %all-gather.4 = f32[16,14,272]{2,1,0:T(8,128)S(1)} all-gather(f32[1,14,272]{2,1,0:T(8,128)S(1)} %maximum_bitcast_fusion.4), channel_id=1, replica_groups=mesh['group'=2,'blk'=16] {'blk'}, dimensions={0}, use_global_device_ids=true | all-gather | bytes 258944 | tf_op jit(solution)/shard_map/all_gather | solution.py:254
  254.1 19.1 %all-gather.5 = f32[16,14,272]{2,1,0:T(8,128)S(1)} all-gather(f32[1,14,272]{2,1,0:T(8,128)S(1)} %maximum_bitcast_fusion.5), channel_id=1, replica_groups=mesh['group'=2,'blk'=16] {'blk'}, dimensions={0}, use_global_device_ids=true | all-gather | bytes 258944 | tf_op jit(solution)/shard_map/all_gather | solution.py:254
  279.2 19.3 %all-gather.6 = f32[16,14,272]{2,1,0:T(8,128)S(1)} all-gather(f32[1,14,272]{2,1,0:T(8,128)S(1)} %maximum_bitcast_fusion.6), channel_id=1, replica_groups=mesh['group'=2,'blk'=16] {'blk'}, dimensions={0}, use_global_device_ids=true | all-gather | bytes 258944 | tf_op jit(solution)/shard_map/all_gather | solution.py:254
  304.4 19.0 %all-gather.7 = f32[16,14,272]{2,1,0:T(8,128)S(1)} all-gather(f32[1,14,272]{2,1,0:T(8,128)S(1)} %maximum_bitcast_fusion.7), channel_id=1, replica_groups=mesh['group'=2,'blk'=16] {'blk'}, dimensions={0}, use_global_device_ids=true | all-gather | bytes 258944 | tf_op jit(solution)/shard_map/all_gather | solution.py:254
  329.6 19.3 %all-gather.8 = f32[16,14,272]{2,1,0:T(8,128)S(1)} all-gather(f32[1,14,272]{2,1,0:T(8,128)S(1)} %maximum_bitcast_fusion.8), channel_id=1, replica_groups=mesh['group'=2,'blk'=16] {'blk'}, dimensions={0}, use_global_device_ids=true | all-gather | bytes 258944 | tf_op jit(solution)/shard_map/all_gather | solution.py:264
  353.3 3.5 all-to-all-start.3
  360.8 3.9 %all-to-all-done.3 = f32[32,8,128]{2,1,0:T(8,128)S(1)} async-done(((f32[32,8,128]{2,1,0:T(8,128)}), f32[32,8,128]{2,1,0:T(8,128)S(1)}, u32[]{:S(2)}, u32[]{:S(2)}) %all-to-all-start.3) | async-done | bytes 131104 | tf_op jit(solution)/shard_map/all_to_all | solution.py:353
  364.7 3.5 all-to-all-start.4
  370.4 5.8 %all-to-all-done.4 = f32[32,8,128]{2,1,0:T(8,128)S(1)} async-done(((f32[32,8,128]{2,1,0:T(8,128)}), f32[32,8,128]{2,1,0:T(8,128)S(1)}, u32[]{:S(2)}, u32[]{:S(2)}) %all-to-all-start.4) | async-done | bytes 131104 | tf_op jit(solution)/shard_map/all_to_all | solution.py:360
  376.8 4.4 %fusion.2 = (f32[4,20,32,128]{3,2,1,0:T(8,128)}, f32[4,20,32,128]{3,2,1,0:T(8,128)}, f32[4,20,32,128]{3,2,1,0:T(8,128)}, f32[4,20,32,128]{3,2,1,0:T(8,128)}) fusion(f32[4,20,32,128]{3,2,1,0:T(8,128)} %constant_dynamic-update-slice_fusion.60, s32[4,32,128]{2,1,0:T(8,128)S(1)} %copy-done.12, f32[4,20,32,128]{3,2,1,0:T(8,128)} %constant_dynamic-update-slice_fusion.40, ...), kind=kLoop, calls=%fused_computation.42 | loop fusion | flops 2293760 | bytes 10682368 | tf_op jit(solution)/shard_map/mul | solution.py:81
  (425 shorter events, 109.8 us)
Async XLA Ops:
  5.0 1.7 copy-start.10
  5.0 2.1 copy-start.11
  5.0 2.1 copy-start.12
  33.4 3.6 copy-start
  33.6 1.1 copy-start.4
  34.7 5.0 %copy-start.2 = (f32[4,20,32,128]{3,2,1,0:T(8,128)}, f32[4,20,32,128]{3,2,1,0:T(8,128)S(1)}, u32[]{:S(2)}) copy-start(f32[4,20,32,128]{3,2,1,0:T(8,128)S(1)} %constant_dynamic-update-slice_fusion.20) | copy-start | bytes 3932164
  43.0 76.6 %all-to-all-start.1 = ((f32[32,8,128]{2,1,0:T(8,128)}), f32[32,8,128]{2,1,0:T(8,128)S(1)}, u32[]{:S(2)}, u32[]{:S(2)}) async-start(f32[32,8,128]{2,1,0:T(8,128)} %scatter_fusion.1), calls=%async_computation.1 | async-start | bytes 262144 | tf_op jit(solution)/shard_map/all_to_all | solution.py:326
  59.2 21.3 %copy-start.22 = (s32[256,8]{0,1:T(8,128)S(1)}, s32[256,8]{0,1:T(8,128)}, u32[]{:S(2)}) copy-start(s32[256,8]{0,1:T(8,128)} %param.14) | copy-start | bytes 24580
  59.3 22.3 %copy-start.1 = (s32[64]{0:T(128)S(1)}, s32[64]{0:T(128)}, u32[]{:S(2)}) copy-start(s32[64]{0:T(128)} %param.12) | copy-start | bytes 772
  82.4 2.2 copy-start.7
  84.7 11.2 %copy-start.6 = (f32[4,20,32,128]{3,2,1,0:T(8,128)S(1)}, f32[4,20,32,128]{3,2,1,0:T(8,128)}, u32[]{:S(2)}) copy-start(f32[4,20,32,128]{3,2,1,0:T(8,128)} %param.17) | copy-start | bytes 3932164
  109.2 2.8 copy-start.18
  112.0 1.1 copy-start.8
  119.6 30.8 %all-to-all-start = ((f32[32,8,128]{2,1,0:T(8,128)}), f32[32,8,128]{2,1,0:T(8,128)S(1)}, u32[]{:S(2)}, u32[]{:S(2)}) async-start(f32[32,8,128]{2,1,0:T(8,128)} %scatter_fusion), calls=%async_computation | async-start | bytes 262144 | tf_op jit(solution)/shard_map/all_to_all | solution.py:319
  150.5 11.4 %all-to-all-start.2 = ((f32[32,8,128]{2,1,0:T(8,128)}), f32[32,8,128]{2,1,0:T(8,128)S(1)}, u32[]{:S(2)}, u32[]{:S(2)}) async-start(f32[32,8,128]{2,1,0:T(8,128)} %scatter_fusion.2), calls=%async_computation.2 | async-start | bytes 262144 | tf_op jit(solution)/shard_map/all_to_all | solution.py:333
  329.1 21.3 %copy-start.13 = (f32[14,8,128]{2,1,0:T(8,128)}, f32[14,8,128]{2,1,0:T(8,128)S(1)}, u32[]{:S(2)}) copy-start(f32[14,8,128]{2,1,0:T(8,128)S(1)} %fusion.89) | copy-start | bytes 172036
  349.0 7.8 %copy-start.19 = (f32[4,1,32,128]{3,2,1,0:T(8,128)S(1)}, f32[4,1,32,128]{3,2,1,0:T(8,128)}, u32[]{:S(2)}) copy-start(f32[4,1,32,128]{3,2,1,0:T(8,128)} %copy-done.18) | copy-start | bytes 196612
  349.0 8.5 %copy-start.17 = (f32[4,1,32,128]{3,2,1,0:T(8,128)S(1)}, f32[4,1,32,128]{3,2,1,0:T(8,128)}, u32[]{:S(2)}) copy-start(f32[4,1,32,128]{3,2,1,0:T(8,128)} %get-tuple-element.174) | copy-start | bytes 196612
  349.0 8.5 %copy-start.20 = (f32[4,1,32,128]{3,2,1,0:T(8,128)S(1)}, f32[4,1,32,128]{3,2,1,0:T(8,128)}, u32[]{:S(2)}) copy-start(f32[4,1,32,128]{3,2,1,0:T(8,128)} %get-tuple-element.119) | copy-start | bytes 196612
  349.0 8.5 %copy-start.21 = (f32[4,1,32,128]{3,2,1,0:T(8,128)S(1)}, f32[4,1,32,128]{3,2,1,0:T(8,128)}, u32[]{:S(2)}) copy-start(f32[4,1,32,128]{3,2,1,0:T(8,128)} %get-tuple-element.175) | copy-start | bytes 196612
  350.4 26.4 %copy-start.5 = (f32[4,20,32,128]{3,2,1,0:T(8,128)S(1)}, f32[4,20,32,128]{3,2,1,0:T(8,128)}, u32[]{:S(2)}) copy-start(f32[4,20,32,128]{3,2,1,0:T(8,128)} %copy-done.4) | copy-start | bytes 3932164
  350.6 26.2 %copy-start.3 = (f32[4,20,32,128]{3,2,1,0:T(8,128)S(1)}, f32[4,20,32,128]{3,2,1,0:T(8,128)}, u32[]{:S(2)}) copy-start(f32[4,20,32,128]{3,2,1,0:T(8,128)} %copy-done.2) | copy-start | bytes 3932164
  353.3 11.4 %all-to-all-start.3 = ((f32[32,8,128]{2,1,0:T(8,128)}), f32[32,8,128]{2,1,0:T(8,128)S(1)}, u32[]{:S(2)}, u32[]{:S(2)}) async-start(f32[32,8,128]{2,1,0:T(8,128)} %scatter_fusion.3), calls=%async_computation.3 | async-start | bytes 262144 | tf_op jit(solution)/shard_map/all_to_all | solution.py:353
  364.7 11.4 %all-to-all-start.4 = ((f32[32,8,128]{2,1,0:T(8,128)}), f32[32,8,128]{2,1,0:T(8,128)S(1)}, u32[]{:S(2)}, u32[]{:S(2)}) async-start(f32[32,8,128]{2,1,0:T(8,128)} %scatter_fusion.4), calls=%async_computation.4 | async-start | bytes 262144 | tf_op jit(solution)/shard_map/all_to_all | solution.py:360
  (4 other events, 3.2 us)
where the time goes:
time: 383 us; the launch traced here: 381 us
  blocking collectives  176 us (46%)
  other arithmetic  88.6 us (23%)
  local copies, waits for them, and re-layouts  73 us (19%)
  starting transfers between devices  23.9 us (6%)
  waiting for transfers between devices  16.9 us (4%)
    all_gather x5, blocking collectives, barotropic(): got_search = lax.all_gather(rim_of(search, 1), 'blk', axis=0, tiled=True)  96 us
    div x4, other arithmetic, stack_mixer(): value = (iteration_number[level] * field[:, level] + lower * value) / denom  44.2 us
    all_gather x1, blocking collectives, barotropic(): lax.all_gather(rim_of(north_tiles, width), 'blk', axis=0, tiled=True)  22.8 us
    all_gather x1, blocking collectives, barotropic(): got_height = lax.all_gather(rim_of(height, 1), 'blk', axis=0, tiled=True)  19.3 us
    all_gather x1, blocking collectives, barotropic(): lax.all_gather(rim_of(zonal_tiles, width), 'blk', axis=0, tiled=True)  19.2 us
    all_gather x1, blocking collectives, barotropic(): lax.all_gather(rim_of(depth_tiles, width), 'blk', axis=0, tiled=True)  19.1 us
    gather x9, local copies, waits for them, and re-layouts, group_rank(): first = jnp.searchsorted(ordered, ordered, side='left')  17.5 us
    scatter x5, local copies, waits for them, and re-layouts, pack_slots(): jnp.zeros((total,) + tiles.shape[1:], tiles.dtype).at[slots]  10.3 us
  transfers between devices with their start and end apart: 5, of which 3 were waited for; matrix products, arithmetic and copies ran while one was open for 20% of the time, Pallas kernels for 0%

commit v1 on v0

v1 whole, which is shorter than its diff:
```python
import functools

import jax
import jax.numpy as jnp
from jax import lax
from jax.experimental import pallas as pl
from jax.experimental.pallas import tpu as pltpu
from jax.sharding import PartitionSpec as P

ITERS = 6
SUB = 4
BLK_DEV = 4
BT_DEV = 14
TILES_DEV = 16
LEVELS = 20
ROWS = 32
COLS = 128
TY = 8
STRIP = 16
PACK = 48

damping = 0.1
coriolis = 0.3
lowest = 0.02
highest = 2.0

STEPS = [1.0 + 0.1 * k for k in range(LEVELS)]
TOTAL = sum(STEPS)
MESH = pl.DeviceIdType.MESH


def chebyshev_plan(count):
    centre = 0.5 * (highest + lowest)
    spread = 0.5 * (highest - lowest)
    sigma = centre / spread
    rho = 1.0 / sigma
    plan = []
    for _ in range(count):
        fresh = 1.0 / (2.0 * sigma - rho)
        plan.append((fresh * rho, 2.0 * fresh / spread))
        rho = fresh
    return (centre, plan)


def lane_of(shape):
    return lax.broadcasted_iota(jnp.int32, shape, 1)


def row_of(shape):
    return lax.broadcasted_iota(jnp.int32, shape, 0)


def side_pack(field, edge):
    lane = lane_of((TY, COLS))
    out = jnp.zeros((TY, COLS), jnp.float32)
    for group in range(SUB):
        rows = field[group * TY : (group + 1) * TY]
        moved = pltpu.roll(rows, (16 + 32 * group) % COLS, 1)
        out = jnp.where(lane // 32 == group, moved, out)
        if edge is not None:
            moved = pltpu.roll(edge[group * TY : (group + 1) * TY], (1 + 32 * group) % COLS, 1)
            out = jnp.where(lane == 32 * group, moved, out)
    return out


def mix_kernel(
    wet_ref, u_ref, v_ref, t_ref, s_ref, k_ref,
    um_ref, vm_ref, tm_ref, sm_ref, div_ref, depth_ref, pack_ref,
    ratio_ref, half_ref, zonal_ref, north_ref,
):
    def strip(index, carry):
        rows = pl.ds(pl.multiple_of(index * STRIP, STRIP), STRIP)
        wet = wet_ref[rows, :]
        zero = jnp.zeros((STRIP, COLS), jnp.float32)
        lower = zero
        lower_half = zero
        ratio = zero
        ratio_half = zero
        mask = (wet > 0).astype(jnp.float32)
        depth = zero
        uv = vv = tv = sv = zero
        for k in range(LEVELS):
            step = STEPS[k]
            depth = depth + step * mask
            u = u_ref[k, rows, :]
            v = v_ref[k, rows, :]
            if k + 1 < LEVELS:
                below = (wet > k + 1).astype(jnp.float32)
                upper = k_ref[k, rows, :] * below
            else:
                below = zero
                upper = zero
            upper_half = 0.5 * upper
            inv = 1.0 / (step + upper + lower * (1.0 - ratio))
            inv_half = 1.0 / (step + upper_half + lower_half * (1.0 - ratio_half))
            scaled = step * mask
            uv = (scaled * (u + coriolis * v) + lower * uv) * inv
            vv = (scaled * (v - coriolis * u) + lower * vv) * inv
            tv = (step * t_ref[k, rows, :] + lower_half * tv) * inv_half
            sv = (step * s_ref[k, rows, :] + lower_half * sv) * inv_half
            ratio = upper * inv
            ratio_half = upper_half * inv_half
            um_ref[k, rows, :] = uv
            vm_ref[k, rows, :] = vv
            tm_ref[k, rows, :] = tv
            sm_ref[k, rows, :] = sv
            ratio_ref[k] = ratio
            half_ref[k] = ratio_half
            lower = upper
            lower_half = upper_half
            mask = below
        last = LEVELS - 1
        zonal = STEPS[last] * uv
        north = STEPS[last] * vv
        mask = (wet > last).astype(jnp.float32)
        tm_ref[last, rows, :] = tv * mask
        sm_ref[last, rows, :] = sv * mask
        for k in range(last - 1, -1, -1):
            ratio = ratio_ref[k]
            ratio_half = half_ref[k]
            uv = um_ref[k, rows, :] + ratio * uv
            vv = vm_ref[k, rows, :] + ratio * vv
            tv = tm_ref[k, rows, :] + ratio_half * tv
            sv = sm_ref[k, rows, :] + ratio_half * sv
            zonal = zonal + STEPS[k] * uv
            north = north + STEPS[k] * vv
            mask = (wet > k).astype(jnp.float32)
            um_ref[k, rows, :] = uv
            vm_ref[k, rows, :] = vv
            tm_ref[k, rows, :] = tv * mask
            sm_ref[k, rows, :] = sv * mask
        zonal_ref[rows, :] = zonal * (1.0 / TOTAL)
        north_ref[rows, :] = north * (1.0 / TOTAL)
        depth_ref[rows, :] = depth * (1.0 / TOTAL)
        return carry

    lax.fori_loop(0, ROWS // STRIP, strip, 0)
    zonal = zonal_ref[...]
    north = north_ref[...]
    depth = depth_ref[...]
    lane = lane_of((ROWS, COLS))
    row = row_of((ROWS, COLS))
    left = jnp.where(lane == 0, 0.0, pltpu.roll(zonal, 1, 1))
    above = jnp.where(row == 0, 0.0, pltpu.roll(north, 1, 0))
    div = zonal - left + north - above
    div_ref[...] = div
    pack_ref[0:8, :] = div[0:8]
    pack_ref[8:16, :] = div[24:32]
    pack_ref[8:9, :] = north[31:32]
    pack_ref[16:24, :] = side_pack(div, zonal)
    pack_ref[24:32, :] = depth[0:8]
    pack_ref[32:40, :] = depth[24:32]
    pack_ref[40:48, :] = side_pack(depth, None)


def column_mix(wet, u, v, t, s, kappa):
    blocks = u.shape[0]
    deep = pl.BlockSpec((None, LEVELS, ROWS, COLS), lambda i: (i, 0, 0, 0))
    flat = pl.BlockSpec((None, ROWS, COLS), lambda i: (i, 0, 0))
    deep_shape = jax.ShapeDtypeStruct(u.shape, jnp.float32)
    flat_shape = jax.ShapeDtypeStruct((blocks, ROWS, COLS), jnp.float32)
    return pl.pallas_call(
        mix_kernel,
        grid=(blocks,),
        in_specs=[flat] + [deep] * 5,
        out_specs=[deep] * 4 + [flat, flat, pl.BlockSpec((None, PACK, COLS), lambda i: (i, 0, 0))],
        out_shape=[deep_shape] * 4
        + [flat_shape, flat_shape, jax.ShapeDtypeStruct((blocks, PACK, COLS), jnp.float32)],
        scratch_shapes=[
            pltpu.VMEM((LEVELS, STRIP, COLS), jnp.float32),
            pltpu.VMEM((LEVELS, STRIP, COLS), jnp.float32),
            pltpu.VMEM((ROWS, COLS), jnp.float32),
            pltpu.VMEM((ROWS, COLS), jnp.float32),
        ],
        compiler_params=pltpu.CompilerParams(vmem_limit_bytes=32 * 2**20),
        name="column_mix",
    )(wet, u, v, t, s, kappa)


def greet(n, me):
    barrier = pltpu.get_barrier_semaphore()

    def one(k, carry):
        pl.semaphore_signal(
            barrier, inc=1, device_id={"blk": lax.rem(me + k, n)}, device_id_type=MESH
        )
        return carry

    lax.fori_loop(1, n, one, 0)
    pl.semaphore_wait(barrier, n - 1)


def gather_kernel(n, x_ref, out_ref, send_sem, recv_sem):
    me = lax.axis_index("blk")
    greet(n, me)

    def copy(k):
        return pltpu.make_async_remote_copy(
            src_ref=x_ref,
            dst_ref=out_ref.at[me],
            send_sem=send_sem.at[k],
            recv_sem=recv_sem.at[k],
            device_id={"blk": lax.rem(me + k, n)},
            device_id_type=MESH,
        )

    def begin(k, carry):
        copy(k).start()
        return carry

    def end(k, carry):
        copy(k).wait()
        return carry

    lax.fori_loop(1, n, begin, 0)
    out_ref[me] = x_ref[...]
    lax.fori_loop(1, n, end, 0)


def gather_packs(n, pack):
    shape = (n,) + pack.shape
    return pl.pallas_call(
        functools.partial(gather_kernel, n),
        out_shape=jax.ShapeDtypeStruct(shape, jnp.float32),
        in_specs=[pl.BlockSpec(memory_space=pltpu.VMEM)],
        out_specs=pl.BlockSpec(memory_space=pltpu.VMEM),
        scratch_shapes=[pltpu.SemaphoreType.DMA((n,)), pltpu.SemaphoreType.DMA((n,))],
        compiler_params=pltpu.CompilerParams(
            collective_id=0, has_side_effects=True, vmem_limit_bytes=32 * 2**20
        ),
        name="gather_packs",
    )(pack)


def spread_kernel(n, cap, place_ref, x_ref, out_ref, held, send_sem, recv_sem):
    me = lax.axis_index("blk")
    greet(n, me)

    def copy(k):
        other = lax.rem(me + k, n)
        return pltpu.make_async_remote_copy(
            src_ref=x_ref.at[other],
            dst_ref=held.at[me],
            send_sem=send_sem.at[k],
            recv_sem=recv_sem.at[k],
            device_id={"blk": other},
            device_id_type=MESH,
        )

    def begin(k, carry):
        copy(k).start()
        return carry

    def end(k, carry):
        copy(k).wait()
        return carry

    lax.fori_loop(1, n, begin, 0)
    held[me] = x_ref[me]
    lax.fori_loop(1, n, end, 0)
    for slot in range(BT_DEV):
        out_ref[slot] = held[place_ref[2 * slot], place_ref[2 * slot + 1]]


def spread_tiles(n, cap, place, tiles):
    return pl.pallas_call(
        functools.partial(spread_kernel, n, cap),
        out_shape=jax.ShapeDtypeStruct((BT_DEV, TY, COLS), jnp.float32),
        in_specs=[
            pl.BlockSpec(memory_space=pltpu.SMEM),
            pl.BlockSpec(memory_space=pltpu.VMEM),
        ],
        out_specs=pl.BlockSpec(memory_space=pltpu.VMEM),
        scratch_shapes=[
            pltpu.VMEM((n, cap, TY, COLS), jnp.float32),
            pltpu.SemaphoreType.DMA((n,)),
            pltpu.SemaphoreType.DMA((n,)),
        ],
        compiler_params=pltpu.CompilerParams(
            collective_id=1, has_side_effects=True, vmem_limit_bytes=32 * 2**20
        ),
        name="spread_tiles",
    )(place, tiles)


def sideways(main, side, amount):
    lane = lane_of(main.shape)
    edge = lane == (0 if amount == 1 else COLS - 1)
    rolled_main = pltpu.roll(main, amount % COLS, 1)
    rolled_side = pltpu.roll(side, amount % COLS, 1)
    return (
        jnp.where(edge, rolled_side, rolled_main),
        jnp.where(edge, rolled_main, rolled_side),
    )


def ring_sum(main, side):
    rows = main.shape[0]

    def vertical(field):
        return field + 0.25 * (pltpu.roll(field, 1, 0) + pltpu.roll(field, rows - 1, 0))

    vm = vertical(main)
    vs = vertical(side)
    lm, ls = sideways(vm, vs, 1)
    rm, rs = sideways(vm, vs, -1)
    return (
        4.0 * (vm - main) + (lm + rm),
        4.0 * (vs - side) + (ls + rs),
    )


def solve_kernel(
    n, cap, runs_ref, owner_ref, near_hbm, gathered, div_ref, depth_ref, wet_ref, um_ref, vm_ref,
    un_ref, vn_ref, out_ref, place_ref,
    near, scalars, counts, sem,
):
    step = pl.program_id(0)
    me = lax.axis_index("blk")

    @pl.when(step == 0)
    def _():
        def find(j, found):
            return jnp.where(runs_ref[j * BLK_DEV] == me, j, found)

        run = lax.fori_loop(0, n, find, 0)
        scalars[0] = run
        copy = pltpu.make_async_copy(
            near_hbm.at[pl.ds(pl.multiple_of(run * TILES_DEV, TILES_DEV), TILES_DEV)], near, sem
        )
        copy.start()

        def clear(j, carry):
            counts[j] = 0
            return carry

        lax.fori_loop(0, n, clear, 0)

        def scan(j, place):
            source = runs_ref[j * BLK_DEV]
            rank = 0
            for a in range(TILES_DEV):
                hit = (owner_ref[j * TILES_DEV + a] == me).astype(jnp.int32)
                place_ref[2 * place] = source
                place_ref[2 * place + 1] = rank
                place = place + hit
                rank = jnp.minimum(rank + hit, cap - 1)
            return place

        lax.fori_loop(0, n, scan, 0)
        copy.wait()

    run = scalars[0]
    base = step * SUB

    def where_is(tile):
        block = tile // SUB
        there = block < n * BLK_DEV
        safe = jnp.where(there, block, 0)
        return (runs_ref[safe], safe % BLK_DEV, there.astype(jnp.float32))

    above = where_is(near[base, 0])
    below = where_is(near[base + SUB - 1, 1])
    above_left = where_is(near[base, 4])
    above_right = where_is(near[base, 5])
    below_left = where_is(near[base + SUB - 1, 6])
    below_right = where_is(near[base + SUB - 1, 7])
    left_tile = near[base, 2]
    right_tile = near[base, 3]
    for a in range(1, SUB):
        left_tile = jnp.minimum(left_tile, near[base + a, 2])
        right_tile = jnp.minimum(right_tile, near[base + a, 3])
    left = where_is(left_tile)
    right = where_is(right_tile)
    own = (me, step, jnp.float32(1.0))

    def load(who, start, rows=TY):
        device, slot, there = who
        return gathered[device, slot, start : start + rows, :] * there

    lane8 = lane_of((TY, COLS))
    row8 = row_of((TY, COLS))

    def corner(who_left, who_right, start):
        mixed = jnp.where(lane8 < TY, load(who_right, start), load(who_left, start))
        return jnp.where((lane8 < TY) | (lane8 >= COLS - TY), mixed, 0.0)

    def beside(start):
        packed = jnp.where(lane8 % 32 >= 16, load(right, start), load(left, start))
        parts = []
        for group in range(SUB):
            moved = pltpu.roll(packed, (112 - 32 * group) % COLS, 1)
            parts.append(jnp.where((lane8 < TY) | (lane8 >= COLS - TY), moved, 0.0))
        return parts

    def edge_column(upper, middle, lower):
        packed = load(middle, 16)
        parts = [pltpu.roll(load(upper, 16), 32, 1)]
        for group in range(SUB):
            moved = packed if group == 0 else pltpu.roll(packed, COLS - 32 * group, 1)
            parts.append(moved)
        parts.append(load(lower, 16))
        return jnp.where(lane48 == 0, jnp.concatenate(parts, axis=0), 0.0)

    lane48 = lane_of((PACK, COLS))
    depth_main = jnp.concatenate([load(above, 32), depth_ref[...], load(below, 24)], axis=0)
    depth_side = jnp.concatenate(
        [corner(above_left, above_right, 32)] + beside(40) + [corner(below_left, below_right, 24)],
        axis=0,
    )
    top_main = load(above, 8)
    top_side = corner(above_left, above_right, 8)
    first_row = row8 == 0
    mid_main = div_ref[...]
    mid_side = beside(16)
    own_main = mid_main[0:8] - jnp.where(first_row, top_main, 0.0)
    mid_side[0] = mid_side[0] - jnp.where(first_row, top_side, 0.0)
    low_main = load(below, 0) - jnp.where(first_row, load(own, 8), 0.0)
    low_side = corner(below_left, below_right, 0) - jnp.where(
        first_row, corner(left, right, 8), 0.0
    )
    div_main = jnp.concatenate([top_main, own_main, mid_main[8:], low_main], axis=0)
    div_side = jnp.concatenate([top_side] + mid_side + [low_side], axis=0)
    div_main = div_main - edge_column(above_left, left, below_left)
    div_side = div_side - edge_column(above, own, below)

    centre, plan = chebyshev_plan(ITERS)
    depths = (depth_main, depth_side)
    divs = (div_main, div_side)
    ocean = [(d > 0).astype(jnp.float32) for d in depths]
    near_ocean = ring_sum(*ocean)
    near_depth = ring_sum(*depths)
    half = [0.5 * o for o in ocean]
    diagonal = [
        damping + h * (d * a + b) for h, d, a, b in zip(half, depths, near_ocean, near_depth)
    ]
    inverse = [1.0 / x for x in diagonal]
    resid = [-(x * o) for x, o in zip(divs, ocean)]
    search = [r * i * (1.0 / centre) for r, i in zip(resid, inverse)]
    height = [search[0], search[1]]
    for it in range(ITERS - 1):
        around = ring_sum(*search)
        weighted = ring_sum(*[d * s for d, s in zip(depths, search)])
        resid = [
            r - (g * s - h * (d * a + b))
            for r, g, s, h, d, a, b in zip(
                resid, diagonal, search, half, depths, around, weighted
            )
        ]
        first, second = plan[it]
        search = [first * s + second * r * i for s, r, i in zip(search, resid, inverse)]
        height = [e + s for e, s in zip(height, search)]
    eta = height[0][TY : TY + ROWS]
    ocean_mid = ocean[0][TY : TY + ROWS]
    eta_east = sideways(height[0], height[1], -1)[0][TY : TY + ROWS]
    ocean_east = sideways(ocean[0], ocean[1], -1)[0][TY : TY + ROWS]
    eta_south = pltpu.roll(height[0], PACK - 1, 0)[TY : TY + ROWS]
    ocean_south = pltpu.roll(ocean[0], PACK - 1, 0)[TY : TY + ROWS]
    east = (eta_east - eta) * ocean_mid * ocean_east
    south = (eta_south - eta) * ocean_mid * ocean_south

    for a in range(SUB):
        target = owner_ref[run * TILES_DEV + base + a]

        @pl.when(target >= 0)
        def _():
            rank = counts[target]
            counts[target] = rank + 1
            out_ref[target, rank] = eta[a * TY : (a + 1) * TY]

    wet = wet_ref[...]
    for k in range(LEVELS):
        wetted = wet > k
        un_ref[k] = jnp.where(wetted, um_ref[k] - east, 0.0)
        vn_ref[k] = jnp.where(wetted, vm_ref[k] - south, 0.0)


def solve(n, cap, patch_owner, piece_owner, neighbours, gathered, div, depth, wet, um, vm):
    blocks = um.shape[0]
    deep = pl.BlockSpec((None, LEVELS, ROWS, COLS), lambda i: (i, 0, 0, 0))
    flat = pl.BlockSpec((None, ROWS, COLS), lambda i: (i, 0, 0))
    deep_shape = jax.ShapeDtypeStruct(um.shape, jnp.float32)
    smem = pl.BlockSpec(memory_space=pltpu.SMEM)
    return pl.pallas_call(
        functools.partial(solve_kernel, n, cap),
        grid=(blocks,),
        in_specs=[
            smem,
            smem,
            pl.BlockSpec(memory_space=pl.ANY),
            pl.BlockSpec(gathered.shape, lambda i: (0, 0, 0, 0)),
            flat,
            flat,
            flat,
            deep,
            deep,
        ],
        out_specs=[deep, deep, pl.BlockSpec((n, cap, TY, COLS), lambda i: (0, 0, 0, 0)), smem],
        out_shape=[
            deep_shape,
            deep_shape,
            jax.ShapeDtypeStruct((n, cap, TY, COLS), jnp.float32),
            jax.ShapeDtypeStruct((2 * BT_DEV + 4,), jnp.int32),
        ],
        scratch_shapes=[
            pltpu.SMEM((TILES_DEV, 8), jnp.int32),
            pltpu.SMEM((1,), jnp.int32),
            pltpu.SMEM((n,), jnp.int32),
            pltpu.SemaphoreType.DMA,
        ],
        compiler_params=pltpu.CompilerParams(vmem_limit_bytes=48 * 2**20),
        name="solve",
    )(patch_owner, piece_owner, neighbours, gathered, div, depth, wet, um, vm)


def on_device(n, wet, patch_owner, piece_owner, neighbours, u, v, t, s, kappa):
    cap = max(2, TILES_DEV // n)
    um, vm, tm, sm, div, depth, pack = column_mix(wet, u, v, t, s, kappa)
    gathered = gather_packs(n, pack)
    un, vn, tiles, place = solve(
        n, cap, patch_owner, piece_owner, neighbours, gathered, div, depth, wet, um, vm
    )
    height = spread_tiles(n, cap, place, tiles)
    return (un, vn, tm, sm, height)


def solution(mesh):
    deep = P(("group", "blk"), None, None, None)
    flat = P(("group", "blk"), None, None)
    return jax.shard_map(
        functools.partial(on_device, mesh.shape["blk"]),
        mesh=mesh,
        in_specs=(flat, P("group"), P("group"), P("group", None)) + (deep,) * 5,
        out_specs=(deep,) * 4 + (flat,),
        check_vma=False,
    )
```

time: 383 us -> 69.5 us (0.18)
  blocking collectives: 176 us -> 0 us
  other arithmetic: 88.6 us -> 0 us
  local copies, waits for them, and re-layouts: 73 us -> 8.87 us
  Pallas kernels: 0 us -> 59.5 us
  starting transfers between devices: 23.9 us -> 0 us
  waiting for transfers between devices: 16.9 us -> 0 us
    all_gather x9 -> x0, blocking collectives: 176 us -> none  [the longest x5 96 us: barotropic(): got_search = lax.all_gather(rim_of(search, 1), 'blk', axis=0, tiled=True)]
    pallas_call x0 -> x4, Pallas kernels: none -> 59.5 us  [the longest x1 32.2 us: gather_packs(): pl.pallas_call(functools.partial(gather_kernel, n), out_shape=jax.ShapeDt...]
    div x8 -> x0, other arithmetic: 46.1 us -> none  [the longest x4 44.2 us: stack_mixer(): value = (iteration_number[level] * field[:, level] + lower * value) / denom]
    gather x31 -> x0, local copies, waits for them, and re-layouts: 32.3 us -> none  [the longest x9 17.5 us: group_rank(): first = jnp.searchsorted(ordered, ordered, side='left')]
    all_to_all x5 -> x0, starting transfers between devices: 23.9 us -> none  [the longest x1 7.36 us: on_device(): lax.all_to_all(pack_slots(north_tiles, send_slot, slot_total), 'blk', spl...]
    all_to_all x5 -> x0, waiting for transfers between devices: 16.9 us -> none  [the longest x1 7.22 us: on_device(): lax.all_to_all(pack_slots(depth_tiles, send_slot, slot_total), 'blk', spl...]
    slice x70 -> x0, local copies, waits for them, and re-layouts: 12.1 us -> none  [the longest x8 7.26 us: crop(): return field[:, width:field.shape[1] - width, width:field.shape[2] - width]]
    scatter x6 -> x0, local copies, waits for them, and re-layouts: 11.9 us -> none  [the longest x5 10.3 us: pack_slots(): jnp.zeros((total,) + tiles.shape[1:], tiles.dtype).at[slots]]
  transfers between devices with their start and end apart: 5 -> 0, of which waited for: 3 -> 0; matrix products, arithmetic and copies ran while one was open for 20% -> 0% of each run, Pallas kernels for 0% -> 0%
where the time goes in v1:
time: 69.5 us; the launch traced here: 69.1 us
  Pallas kernels  59.5 us (86%)
  local copies, waits for them, and re-layouts  8.87 us (13%)
  between operations  0.7 us (1%)
    pallas_call x1, Pallas kernels, gather_packs(): pl.pallas_call(functools.partial(gather_kernel, n), out_shape=jax.ShapeDt...  32.2 us
    pallas_call x1, Pallas kernels, spread_tiles(): pl.pallas_call(functools.partial(spread_kernel, n, cap), out_shape=jax.Sh...  16.3 us
    unnamed x20, local copies, waits for them, and re-layouts  8.87 us
    pallas_call x1, Pallas kernels, solve(): pl.pallas_call(functools.partial(solve_kernel, n, cap), grid=(blocks,), i...  7.2 us
    pallas_call x1, Pallas kernels, column_mix(): pl.pallas_call(mix_kernel, grid=(blocks,), in_specs=[flat] + [deep] * 5,...  3.79 us

profile of v1, /device:TPU:0, one launch (start us, length us, event | category | flops | bytes accessed | tf_op | source)
XLA Modules:
  0.0 69.1 jit_solution(5320109203479227991)
XLA Ops:
  0.6 0.8 %copy.14.near_hbm = s32[256,8]{1,0:T(8,128)S(1)} copy(s32[256,8]{0,1:T(8,128)} %param.12) | data formatting | bytes 16384 | tf_op args[3]
  1.5 0.0 copy-start
  1.5 1.3 %copy-done = f32[4,20,32,128]{3,2,1,0:T(8,128)S(1)} copy-done((f32[4,20,32,128]{3,2,1,0:T(8,128)S(1)}, f32[4,20,32,128]{3,2,1,0:T(8,128)}, u32[]{:S(2)}) %copy-start) | copy-done | bytes 1310744
  2.8 0.0 copy-start.1
  2.8 1.3 %copy-done.1 = f32[4,20,32,128]{3,2,1,0:T(8,128)S(1)} copy-done((f32[4,20,32,128]{3,2,1,0:T(8,128)S(1)}, f32[4,20,32,128]{3,2,1,0:T(8,128)}, u32[]{:S(2)}) %copy-start.1) | copy-done | bytes 1310744
  4.1 0.0 copy-start.2
  4.1 1.3 %copy-done.2 = f32[4,20,32,128]{3,2,1,0:T(8,128)S(1)} copy-done((f32[4,20,32,128]{3,2,1,0:T(8,128)S(1)}, f32[4,20,32,128]{3,2,1,0:T(8,128)}, u32[]{:S(2)}) %copy-start.2) | copy-done | bytes 1310744
  5.4 0.0 copy-start.3
  5.4 1.3 %copy-done.3 = f32[4,20,32,128]{3,2,1,0:T(8,128)S(1)} copy-done((f32[4,20,32,128]{3,2,1,0:T(8,128)S(1)}, f32[4,20,32,128]{3,2,1,0:T(8,128)}, u32[]{:S(2)}) %copy-start.3) | copy-done | bytes 1310744
  6.7 0.0 copy-start.4
  6.7 1.3 %copy-done.4 = f32[4,20,32,128]{3,2,1,0:T(8,128)S(1)} copy-done((f32[4,20,32,128]{3,2,1,0:T(8,128)S(1)}, f32[4,20,32,128]{3,2,1,0:T(8,128)}, u32[]{:S(2)}) %copy-start.4) | copy-done | bytes 1310744
  8.0 0.0 copy-start.5
  8.0 0.8 %copy-done.5 = s32[4,32,128]{2,1,0:T(8,128)S(1)} copy-done((s32[4,32,128]{2,1,0:T(8,128)S(1)}, s32[4,32,128]{2,1,0:T(8,128)}, u32[]{:S(2)}) %copy-start.5) | copy-done | bytes 65560
  8.9 3.8 %column_mix.1 = (f32[4,20,32,128]{3,2,1,0:T(8,128)S(1)}, f32[4,20,32,128]{3,2,1,0:T(8,128)S(1)}, f32[4,20,32,128]{3,2,1,0:T(8,128)}, f32[4,20,32,128]{3,2,1,0:T(...) custom-call(s32[4,32,128]{2,1,0:T(8,128)S(1)} %copy-done.5, ...), custom_call_target="tpu_custom_call" | custom-call | tf_op jit(solution)/shard_map/column_mix/pallas_call | solution.py:162
  12.7 0.0 copy-start.6
  12.7 0.0 copy-start.7
  12.7 0.0 copy-start.8
  12.7 32.2 %gather_packs.1.gathered = f32[16,4,48,128]{3,2,1,0:T(8,128)S(1)} custom-call(f32[4,48,128]{2,1,0:T(8,128)S(1)} %get-tuple-element.16.x_ref), custom_call_target="tpu_custom_call" | custom-call | tf_op jit(solution)/shard_map/gather_packs/pallas_call | solution.py:222
  44.9 0.0 copy-done.6
  44.9 0.0 copy-done.7
  44.9 0.0 copy-done.8
  44.9 7.2 %solve.1 = (f32[4,20,32,128]{3,2,1,0:T(8,128)}, f32[4,20,32,128]{3,2,1,0:T(8,128)}, f32[16,2,8,128]{3,2,1,0:T(8,128)S(1)}, s32[32]{0:T(128)S(1)}) custom-call(s32[64]{0:T(128)S(1)} %copy-done.8, s32[256]{0:T(256)S(1)} %copy-done.7, s32[256,8]{1,0:T(8,128)S(1)} %copy.14.near_hbm, f32[16,4,48,128]{3,2,1,0:T(8,128)S(1)} %gather_packs.1.gathered, ...), custom_call_target="tpu_custom_call" | custom-call | tf_op jit(solution)/shard_map/solve/pallas_call | solution.py:484
  52.1 16.3 %spread_tiles.1 = f32[14,8,128]{2,1,0:T(8,128)S(1)} custom-call(s32[32]{0:T(128)S(1)} %get-tuple-element.25.place_ref, f32[16,2,8,128]{3,2,1,0:T(8,128)S(1)} %get-tuple-element.26.x_ref), custom_call_target="tpu_custom_call" | custom-call | tf_op jit(solution)/shard_map/spread_tiles/pallas_call | solution.py:266
  68.5 0.6 copy.16
Async XLA Ops:
  1.5 1.3 %copy-start = (f32[4,20,32,128]{3,2,1,0:T(8,128)S(1)}, f32[4,20,32,128]{3,2,1,0:T(8,128)}, u32[]{:S(2)}) copy-start(f32[4,20,32,128]{3,2,1,0:T(8,128)} %u_ref.1) | copy-start | bytes 3932164
  2.8 1.3 %copy-start.1 = (f32[4,20,32,128]{3,2,1,0:T(8,128)S(1)}, f32[4,20,32,128]{3,2,1,0:T(8,128)}, u32[]{:S(2)}) copy-start(f32[4,20,32,128]{3,2,1,0:T(8,128)} %v_ref.1) | copy-start | bytes 3932164
  4.1 1.3 %copy-start.2 = (f32[4,20,32,128]{3,2,1,0:T(8,128)S(1)}, f32[4,20,32,128]{3,2,1,0:T(8,128)}, u32[]{:S(2)}) copy-start(f32[4,20,32,128]{3,2,1,0:T(8,128)} %t_ref.1) | copy-start | bytes 3932164
  5.4 1.3 %copy-start.3 = (f32[4,20,32,128]{3,2,1,0:T(8,128)S(1)}, f32[4,20,32,128]{3,2,1,0:T(8,128)}, u32[]{:S(2)}) copy-start(f32[4,20,32,128]{3,2,1,0:T(8,128)} %s_ref.1) | copy-start | bytes 3932164
  6.7 1.3 %copy-start.4 = (f32[4,20,32,128]{3,2,1,0:T(8,128)S(1)}, f32[4,20,32,128]{3,2,1,0:T(8,128)}, u32[]{:S(2)}) copy-start(f32[4,20,32,128]{3,2,1,0:T(8,128)} %k_ref.1) | copy-start | bytes 3932164
  8.0 0.8 %copy-start.5 = (s32[4,32,128]{2,1,0:T(8,128)S(1)}, s32[4,32,128]{2,1,0:T(8,128)}, u32[]{:S(2)}) copy-start(s32[4,32,128]{2,1,0:T(8,128)} %wet_ref.3) | copy-start | bytes 196612
  12.7 32.2 %copy-start.6 = (s32[4,32,128]{2,1,0:T(8,128)S(1)}, s32[4,32,128]{2,1,0:T(8,128)}, u32[]{:S(2)}) copy-start(s32[4,32,128]{2,1,0:T(8,128)} %wet_ref.3) | copy-start | bytes 196612
  12.7 32.2 %copy-start.7 = (s32[256]{0:T(256)S(1)}, s32[256]{0:T(256)}, u32[]{:S(2)}) copy-start(s32[256]{0:T(256)} %owner_ref.1) | copy-start | bytes 3076
  12.7 32.2 %copy-start.8 = (s32[64]{0:T(128)S(1)}, s32[64]{0:T(128)}, u32[]{:S(2)}) copy-start(s32[64]{0:T(128)} %runs_ref.1) | copy-start | bytes 772

commit v2 on v1

v2 whole, which is shorter than its diff:
```python
import functools

import jax
import jax.numpy as jnp
from jax import lax
from jax.experimental import pallas as pl
from jax.experimental.pallas import tpu as pltpu
from jax.sharding import PartitionSpec as P

ITERS = 6
SUB = 4
BLK_DEV = 4
BT_DEV = 14
TILES_DEV = 16
LEVELS = 20
ROWS = 32
COLS = 128
TY = 8
STRIP = 16
PACK = 24
TALL = 48

damping = 0.1
coriolis = 0.3
lowest = 0.02
highest = 2.0

STEPS = [1.0 + 0.1 * k for k in range(LEVELS)]
TOTAL = sum(STEPS)
MESH = pl.DeviceIdType.MESH


def chebyshev_plan(count):
    centre = 0.5 * (highest + lowest)
    spread = 0.5 * (highest - lowest)
    sigma = centre / spread
    rho = 1.0 / sigma
    plan = []
    for _ in range(count):
        fresh = 1.0 / (2.0 * sigma - rho)
        plan.append((fresh * rho, 2.0 * fresh / spread))
        rho = fresh
    return (centre, plan)


def lane_of(shape):
    return lax.broadcasted_iota(jnp.int32, shape, 1)


def row_of(shape):
    return lax.broadcasted_iota(jnp.int32, shape, 0)


def side_pack(field, edge):
    lane = lane_of((TY, COLS))
    out = jnp.zeros((TY, COLS), jnp.float32)
    for group in range(SUB):
        rows = field[group * TY : (group + 1) * TY]
        moved = pltpu.roll(rows, (16 + 32 * group) % COLS, 1)
        out = jnp.where(lane // 32 == group, moved, out)
        if edge is not None:
            moved = pltpu.roll(edge[group * TY : (group + 1) * TY], (1 + 32 * group) % COLS, 1)
            out = jnp.where(lane == 32 * group, moved, out)
    return out


def scalars_mix_kernel(wet_ref, t_ref, s_ref, k_ref, tm_ref, sm_ref, half_ref):
    def strip(index, carry):
        rows = pl.ds(pl.multiple_of(index * STRIP, STRIP), STRIP)
        wet = wet_ref[rows, :]
        zero = jnp.zeros((STRIP, COLS), jnp.float32)
        lower = ratio = tv = sv = zero
        for k in range(LEVELS):
            step = STEPS[k]
            if k + 1 < LEVELS:
                upper = jnp.where(wet > k + 1, 0.5 * k_ref[k, rows, :], 0.0)
            else:
                upper = zero
            inv = 1.0 / (step + upper + lower * (1.0 - ratio))
            tv = (step * t_ref[k, rows, :] + lower * tv) * inv
            sv = (step * s_ref[k, rows, :] + lower * sv) * inv
            ratio = upper * inv
            tm_ref[k, rows, :] = tv
            sm_ref[k, rows, :] = sv
            half_ref[k] = ratio
            lower = upper
        last = LEVELS - 1
        tm_ref[last, rows, :] = jnp.where(wet > last, tv, 0.0)
        sm_ref[last, rows, :] = jnp.where(wet > last, sv, 0.0)
        for k in range(last - 1, -1, -1):
            ratio = half_ref[k]
            tv = tm_ref[k, rows, :] + ratio * tv
            sv = sm_ref[k, rows, :] + ratio * sv
            tm_ref[k, rows, :] = jnp.where(wet > k, tv, 0.0)
            sm_ref[k, rows, :] = jnp.where(wet > k, sv, 0.0)
        return carry

    lax.fori_loop(0, ROWS // STRIP, strip, 0)


def scalars_mix(wet, t, s, kappa):
    blocks = t.shape[0]
    deep = pl.BlockSpec((None, LEVELS, ROWS, COLS), lambda i: (i, 0, 0, 0))
    flat = pl.BlockSpec((None, ROWS, COLS), lambda i: (i, 0, 0))
    return pl.pallas_call(
        scalars_mix_kernel,
        grid=(blocks,),
        in_specs=[flat, deep, deep, deep],
        out_specs=[deep, deep],
        out_shape=[jax.ShapeDtypeStruct(t.shape, jnp.float32)] * 2,
        scratch_shapes=[pltpu.VMEM((LEVELS, STRIP, COLS), jnp.float32)],
        compiler_params=pltpu.CompilerParams(vmem_limit_bytes=24 * 2**20),
        name="scalars_mix",
    )(wet, t, s, kappa)


def greet(n, me):
    barrier = pltpu.get_barrier_semaphore()

    def one(k, carry):
        pl.semaphore_signal(
            barrier, inc=1, device_id={"blk": lax.rem(me + k, n)}, device_id_type=MESH
        )
        return carry

    lax.fori_loop(1, n, one, 0)
    pl.semaphore_wait(barrier, n - 1)


class Relay:
    def __init__(self, n, me, x_ref, out_ref, send_sem, recv_sem):
        self.me, self.x, self.out = me, x_ref, out_ref
        self.send_sem, self.recv_sem = send_sem, recv_sem
        self.sent = []
        depth = n // 4
        z, y, c = me // 4, (me // 2) % 2, me % 2

        def at(z, y, c):
            return (z * 2 + y) * 2 + c

        hops = sorted(range(1, depth), key=lambda k: min(k, depth - k))
        far = [lax.rem(z + k, depth) for k in hops]
        self.line = [at(f, y, c) for f in far]
        self.y_peer = at(z, 1 - y, c)
        self.sibling = at(z, y, 1 - c)
        self.cross = [self.y_peer] + [at(f, 1 - y, c) for f in far]
        self.rest = [self.sibling] + [at(f, y, 1 - c) for f in far]
        self.rest += [at(f, 1 - y, 1 - c) for f in [z] + far]
        self.peers = self.line + [self.y_peer, self.sibling]

    def copy(self, source, device, slot, first):
        return pltpu.make_async_remote_copy(
            src_ref=self.x if first else self.out.at[source],
            dst_ref=self.out.at[source],
            send_sem=self.send_sem.at[slot],
            recv_sem=self.recv_sem.at[source],
            device_id={"blk": device},
            device_id_type=MESH,
        )

    def send(self, source, device, first=False):
        copy = self.copy(source, device, len(self.sent), first)
        copy.start()
        self.sent.append(copy)

    def arrived(self, source):
        self.copy(source, self.sibling, 0, False).wait_recv()

    def start(self):
        for peer in self.peers:
            self.send(self.me, peer, True)
        self.out[self.me] = self.x[...]

    def second(self):
        for source in self.line:
            self.arrived(source)
            self.send(source, self.y_peer)
            self.send(source, self.sibling)

    def third(self):
        for source in self.cross:
            self.arrived(source)
            self.send(source, self.sibling)

    def finish(self):
        for source in self.rest:
            self.arrived(source)
        for copy in self.sent:
            copy.wait_send()


def flow_kernel(
    n, wet_hbm, u_hbm, v_hbm, k_hbm,
    um_ref, vm_ref, div_ref, depth_ref, got_div, got_depth,
    wet_ref, u_ref, v_ref, k_ref, ratio_ref, zonal_ref, north_ref, div_pack, depth_pack,
    wet_sem, u_sem, v_sem, k_sem, div_send, div_recv, depth_send, depth_recv,
):
    me = lax.axis_index("blk")
    relay_depth = Relay(n, me, depth_pack, got_depth, depth_send, depth_recv)
    relay_div = Relay(n, me, div_pack, got_div, div_send, div_recv)
    barrier = pltpu.get_barrier_semaphore()
    for peer in relay_depth.peers:
        pl.semaphore_signal(barrier, inc=1, device_id={"blk": peer}, device_id_type=MESH)
    wet_copy = pltpu.make_async_copy(wet_hbm, wet_ref, wet_sem)
    wet_copy.start()

    def fetch(block):
        return [
            pltpu.make_async_copy(hbm.at[block], ref.at[block], sem.at[block])
            for hbm, ref, sem in ((u_hbm, u_ref, u_sem), (v_hbm, v_ref, v_sem), (k_hbm, k_ref, k_sem))
        ]

    for block in range(BLK_DEV):
        for copy in fetch(block):
            copy.start()
    wet_copy.wait()
    for block in range(BLK_DEV):
        count = wet_ref[block].astype(jnp.float32)
        depth = (count + 0.05 * (count * (count - 1.0))) * (1.0 / TOTAL)
        depth_ref[block] = depth
        depth_pack[block, 0:8] = depth[0:8]
        depth_pack[block, 8:16] = depth[24:32]
        depth_pack[block, 16:24] = side_pack(depth, None)
    pl.semaphore_wait(barrier, len(relay_depth.peers))
    relay_depth.start()

    def one_block(block, carry):
        for copy in fetch(block):
            copy.wait()

        def strip(index, inner):
            rows = pl.ds(pl.multiple_of(index * STRIP, STRIP), STRIP)
            wet = wet_ref[block, rows, :]
            zero = jnp.zeros((STRIP, COLS), jnp.float32)
            lower = ratio = uv = vv = zero
            for k in range(LEVELS):
                step = STEPS[k]
                u = u_ref[block, k, rows, :]
                v = v_ref[block, k, rows, :]
                if k + 1 < LEVELS:
                    upper = jnp.where(wet > k + 1, k_ref[block, k, rows, :], 0.0)
                else:
                    upper = zero
                inv = 1.0 / (step + upper + lower * (1.0 - ratio))
                scaled = jnp.where(wet > k, step, 0.0)
                uv = (scaled * (u + coriolis * v) + lower * uv) * inv
                vv = (scaled * (v - coriolis * u) + lower * vv) * inv
                ratio = upper * inv
                um_ref[block, k, rows, :] = uv
                vm_ref[block, k, rows, :] = vv
                ratio_ref[k] = ratio
                lower = upper
            last = LEVELS - 1
            zonal = STEPS[last] * uv
            north = STEPS[last] * vv
            for k in range(last - 1, -1, -1):
                ratio = ratio_ref[k]
                uv = um_ref[block, k, rows, :] + ratio * uv
                vv = vm_ref[block, k, rows, :] + ratio * vv
                zonal = zonal + STEPS[k] * uv
                north = north + STEPS[k] * vv
                um_ref[block, k, rows, :] = uv
                vm_ref[block, k, rows, :] = vv
            zonal_ref[rows, :] = zonal * (1.0 / TOTAL)
            north_ref[rows, :] = north * (1.0 / TOTAL)
            return inner

        lax.fori_loop(0, ROWS // STRIP, strip, 0)
        zonal = zonal_ref[...]
        north = north_ref[...]
        lane = lane_of((ROWS, COLS))
        row = row_of((ROWS, COLS))
        left = jnp.where(lane == 0, 0.0, pltpu.roll(zonal, 1, 1))
        above = jnp.where(row == 0, 0.0, pltpu.roll(north, 1, 0))
        div = zonal - left + north - above
        div_ref[block] = div
        div_pack[block, 0:8] = div[0:8]
        div_pack[block, 8:16] = jnp.where(
            row_of((TY, COLS)) == 0, pltpu.roll(north[24:32], 1, 0), div[24:32]
        )
        div_pack[block, 16:24] = side_pack(div, zonal)
        return carry

    lax.fori_loop(0, BLK_DEV, one_block, 0)
    relay_div.start()
    relay_depth.second()
    relay_depth.third()
    relay_div.second()
    relay_div.third()
    relay_depth.finish()
    relay_div.finish()


def flow(n, wet, u, v, kappa):
    blocks = u.shape[0]
    deep = jax.ShapeDtypeStruct(u.shape, jnp.float32)
    flat = jax.ShapeDtypeStruct((blocks, ROWS, COLS), jnp.float32)
    got = jax.ShapeDtypeStruct((n, blocks, PACK, COLS), jnp.float32)
    vmem = pl.BlockSpec(memory_space=pltpu.VMEM)
    hbm = pl.BlockSpec(memory_space=pltpu.MemorySpace.HBM)
    pack = pltpu.VMEM((blocks, PACK, COLS), jnp.float32)
    return pl.pallas_call(
        functools.partial(flow_kernel, n),
        in_specs=[hbm] * 4,
        out_specs=[vmem] * 6,
        out_shape=[deep, deep, flat, flat, got, got],
        scratch_shapes=[
            pltpu.VMEM(wet.shape, jnp.int32),
            pltpu.VMEM(u.shape, jnp.float32),
            pltpu.VMEM(u.shape, jnp.float32),
            pltpu.VMEM(u.shape, jnp.float32),
            pltpu.VMEM((LEVELS, STRIP, COLS), jnp.float32),
            pltpu.VMEM((ROWS, COLS), jnp.float32),
            pltpu.VMEM((ROWS, COLS), jnp.float32),
            pack,
            pack,
            pltpu.SemaphoreType.DMA,
        ]
        + [pltpu.SemaphoreType.DMA((blocks,))] * 3
        + [pltpu.SemaphoreType.DMA((n,))] * 4,
        compiler_params=pltpu.CompilerParams(
            collective_id=0, has_side_effects=True, vmem_limit_bytes=28 * 2**20
        ),
        name="flow",
    )(wet, u, v, kappa)


def spread_kernel(n, cap, place_ref, x_ref, out_ref, held, send_sem, recv_sem):
    me = lax.axis_index("blk")
    greet(n, me)

    def copy(k):
        other = lax.rem(me + k, n)
        return pltpu.make_async_remote_copy(
            src_ref=x_ref.at[other],
            dst_ref=held.at[me],
            send_sem=send_sem.at[k],
            recv_sem=recv_sem.at[k],
            device_id={"blk": other},
            device_id_type=MESH,
        )

    def begin(k, carry):
        copy(k).start()
        return carry

    def end(k, carry):
        copy(k).wait()
        return carry

    lax.fori_loop(1, n, begin, 0)
    held[me] = x_ref[me]
    lax.fori_loop(1, n, end, 0)
    for slot in range(BT_DEV):
        out_ref[slot] = held[place_ref[2 * slot], place_ref[2 * slot + 1]]


def spread_tiles(n, cap, place, tiles):
    return pl.pallas_call(
        functools.partial(spread_kernel, n, cap),
        out_shape=jax.ShapeDtypeStruct((BT_DEV, TY, COLS), jnp.float32),
        in_specs=[
            pl.BlockSpec(memory_space=pltpu.SMEM),
            pl.BlockSpec(memory_space=pltpu.VMEM),
        ],
        out_specs=pl.BlockSpec(memory_space=pltpu.VMEM),
        scratch_shapes=[
            pltpu.VMEM((n, cap, TY, COLS), jnp.float32),
            pltpu.SemaphoreType.DMA((n,)),
            pltpu.SemaphoreType.DMA((n,)),
        ],
        compiler_params=pltpu.CompilerParams(
            collective_id=1, has_side_effects=True, vmem_limit_bytes=32 * 2**20
        ),
        name="spread_tiles",
    )(place, tiles)


def sideways(main, side, amount):
    lane = lane_of(main.shape)
    edge = lane == (0 if amount == 1 else COLS - 1)
    rolled_main = pltpu.roll(main, amount % COLS, 1)
    rolled_side = pltpu.roll(side, amount % COLS, 1)
    return (
        jnp.where(edge, rolled_side, rolled_main),
        jnp.where(edge, rolled_main, rolled_side),
    )


def ring_sum(main, side):
    rows = main.shape[0]

    def vertical(field):
        return field + 0.25 * (pltpu.roll(field, 1, 0) + pltpu.roll(field, rows - 1, 0))

    vm = vertical(main)
    vs = vertical(side)
    lm, ls = sideways(vm, vs, 1)
    rm, rs = sideways(vm, vs, -1)
    return (
        4.0 * (vm - main) + (lm + rm),
        4.0 * (vs - side) + (ls + rs),
    )


def solve_kernel(
    n, cap, runs_ref, owner_ref, near, got_div, got_depth, div_ref, depth_ref, wet_ref, um_ref, vm_ref,
    un_ref, vn_ref, out_ref, place_ref,
    scalars, counts,
):
    step = pl.program_id(0)
    me = lax.axis_index("blk")

    @pl.when(step == 0)
    def _():
        def find(j, found):
            return jnp.where(runs_ref[j * BLK_DEV] == me, j, found)

        run = lax.fori_loop(0, n, find, 0)
        scalars[0] = run
        def clear(j, carry):
            counts[j] = 0
            return carry

        lax.fori_loop(0, n, clear, 0)

        def scan(j, place):
            source = runs_ref[j * BLK_DEV]
            rank = 0
            for a in range(TILES_DEV):
                hit = (owner_ref[j * TILES_DEV + a] == me).astype(jnp.int32)
                place_ref[2 * place] = source
                place_ref[2 * place + 1] = rank
                place = place + hit
                rank = jnp.minimum(rank + hit, cap - 1)
            return place

        lax.fori_loop(0, n, scan, 0)

    run = scalars[0]
    base = step * SUB

    def where_is(tile):
        block = tile // SUB
        there = block < n * BLK_DEV
        safe = jnp.where(there, block, 0)
        return (runs_ref[safe], safe % BLK_DEV, there.astype(jnp.float32))

    first = run * TILES_DEV + base
    final = first + SUB - 1
    above = where_is(near[0, first])
    below = where_is(near[1, final])
    above_left = where_is(near[4, first])
    above_right = where_is(near[5, first])
    below_left = where_is(near[6, final])
    below_right = where_is(near[7, final])
    left_tile = near[2, first]
    right_tile = near[3, first]
    for a in range(1, SUB):
        left_tile = jnp.minimum(left_tile, near[2, first + a])
        right_tile = jnp.minimum(right_tile, near[3, first + a])
    left = where_is(left_tile)
    right = where_is(right_tile)
    own = (me, step, jnp.float32(1.0))

    def load(got, who, start):
        device, slot, there = who
        return got[device, slot, start : start + TY, :] * there

    lane8 = lane_of((TY, COLS))
    row8 = row_of((TY, COLS))

    def corner(got, who_left, who_right, start):
        mixed = jnp.where(lane8 < TY, load(got, who_right, start), load(got, who_left, start))
        return jnp.where((lane8 < TY) | (lane8 >= COLS - TY), mixed, 0.0)

    def beside(got):
        packed = jnp.where(lane8 % 32 >= 16, load(got, right, 16), load(got, left, 16))
        parts = []
        for group in range(SUB):
            moved = pltpu.roll(packed, (112 - 32 * group) % COLS, 1)
            parts.append(jnp.where((lane8 < TY) | (lane8 >= COLS - TY), moved, 0.0))
        return parts

    def edge_column(upper, middle, lower):
        packed = load(got_div, middle, 16)
        parts = [pltpu.roll(load(got_div, upper, 16), 32, 1)]
        for group in range(SUB):
            moved = packed if group == 0 else pltpu.roll(packed, COLS - 32 * group, 1)
            parts.append(moved)
        parts.append(load(got_div, lower, 16))
        return jnp.where(lane48 == 0, jnp.concatenate(parts, axis=0), 0.0)

    lane48 = lane_of((TALL, COLS))
    depth_main = jnp.concatenate(
        [load(got_depth, above, 8), depth_ref[...], load(got_depth, below, 0)], axis=0
    )
    depth_side = jnp.concatenate(
        [corner(got_depth, above_left, above_right, 8)]
        + beside(got_depth)
        + [corner(got_depth, below_left, below_right, 0)],
        axis=0,
    )
    top_main = load(got_div, above, 8)
    top_side = corner(got_div, above_left, above_right, 8)
    first_row = row8 == 0
    mid_main = div_ref[...]
    mid_side = beside(got_div)
    own_main = mid_main[0:8] - jnp.where(first_row, top_main, 0.0)
    mid_side[0] = mid_side[0] - jnp.where(first_row, top_side, 0.0)
    low_main = load(got_div, below, 0) - jnp.where(first_row, load(got_div, own, 8), 0.0)
    low_side = corner(got_div, below_left, below_right, 0) - jnp.where(
        first_row, corner(got_div, left, right, 8), 0.0
    )
    div_main = jnp.concatenate([top_main, own_main, mid_main[8:], low_main], axis=0)
    div_side = jnp.concatenate([top_side] + mid_side + [low_side], axis=0)
    div_main = div_main - edge_column(above_left, left, below_left)
    div_side = div_side - edge_column(above, own, below)

    centre, plan = chebyshev_plan(ITERS)
    depths = (depth_main, depth_side)
    divs = (div_main, div_side)
    ocean = [(d > 0).astype(jnp.float32) for d in depths]
    near_ocean = ring_sum(*ocean)
    near_depth = ring_sum(*depths)
    half = [0.5 * o for o in ocean]
    diagonal = [
        damping + h * (d * a + b) for h, d, a, b in zip(half, depths, near_ocean, near_depth)
    ]
    inverse = [1.0 / x for x in diagonal]
    resid = [-(x * o) for x, o in zip(divs, ocean)]
    search = [r * i * (1.0 / centre) for r, i in zip(resid, inverse)]
    height = [search[0], search[1]]
    for it in range(ITERS - 1):
        around = ring_sum(*search)
        weighted = ring_sum(*[d * s for d, s in zip(depths, search)])
        resid = [
            r - (g * s - h * (d * a + b))
            for r, g, s, h, d, a, b in zip(
                resid, diagonal, search, half, depths, around, weighted
            )
        ]
        first, second = plan[it]
        search = [first * s + second * r * i for s, r, i in zip(search, resid, inverse)]
        height = [e + s for e, s in zip(height, search)]
    eta = height[0][TY : TY + ROWS]
    ocean_mid = ocean[0][TY : TY + ROWS]
    eta_east = sideways(height[0], height[1], -1)[0][TY : TY + ROWS]
    ocean_east = sideways(ocean[0], ocean[1], -1)[0][TY : TY + ROWS]
    eta_south = pltpu.roll(height[0], TALL - 1, 0)[TY : TY + ROWS]
    ocean_south = pltpu.roll(ocean[0], TALL - 1, 0)[TY : TY + ROWS]
    east = (eta_east - eta) * ocean_mid * ocean_east
    south = (eta_south - eta) * ocean_mid * ocean_south

    for a in range(SUB):
        target = owner_ref[run * TILES_DEV + base + a]

        @pl.when(target >= 0)
        def _():
            rank = counts[target]
            counts[target] = rank + 1
            out_ref[target, rank] = eta[a * TY : (a + 1) * TY]

    wet = wet_ref[...]
    for k in range(LEVELS):
        wetted = wet > k
        un_ref[k] = jnp.where(wetted, um_ref[k] - east, 0.0)
        vn_ref[k] = jnp.where(wetted, vm_ref[k] - south, 0.0)


def solve(n, cap, patch_owner, piece_owner, near, got_div, got_depth, div, depth, wet, um, vm):
    blocks = um.shape[0]
    deep = pl.BlockSpec((None, LEVELS, ROWS, COLS), lambda i: (i, 0, 0, 0))
    flat = pl.BlockSpec((None, ROWS, COLS), lambda i: (i, 0, 0))
    deep_shape = jax.ShapeDtypeStruct(um.shape, jnp.float32)
    smem = pl.BlockSpec(memory_space=pltpu.SMEM)
    return pl.pallas_call(
        functools.partial(solve_kernel, n, cap),
        grid=(blocks,),
        in_specs=[
            smem,
            smem,
            smem,
            pl.BlockSpec(memory_space=pltpu.VMEM),
            pl.BlockSpec(memory_space=pltpu.VMEM),
            flat,
            flat,
            flat,
            deep,
            deep,
        ],
        out_specs=[deep, deep, pl.BlockSpec((n, cap, TY, COLS), lambda i: (0, 0, 0, 0)), smem],
        out_shape=[
            deep_shape,
            deep_shape,
            jax.ShapeDtypeStruct((n, cap, TY, COLS), jnp.float32),
            jax.ShapeDtypeStruct((2 * BT_DEV + 4,), jnp.int32),
        ],
        scratch_shapes=[
            pltpu.SMEM((1,), jnp.int32),
            pltpu.SMEM((n,), jnp.int32),
        ],
        compiler_params=pltpu.CompilerParams(vmem_limit_bytes=48 * 2**20),
        name="solve",
    )(patch_owner, piece_owner, near, got_div, got_depth, div, depth, wet, um, vm)


def on_device(n, wet, patch_owner, piece_owner, neighbours, u, v, t, s, kappa):
    cap = max(2, TILES_DEV // n)
    um, vm, div, depth, got_div, got_depth = flow(n, wet, u, v, kappa)
    tm, sm = scalars_mix(wet, t, s, kappa)
    un, vn, tiles, place = solve(
        n, cap, patch_owner, piece_owner, neighbours.T,
        got_div, got_depth, div, depth, wet, um, vm,
    )
    height = spread_tiles(n, cap, place, tiles)
    return (un, vn, tm, sm, height)


def solution(mesh):
    deep = P(("group", "blk"), None, None, None)
    flat = P(("group", "blk"), None, None)
    return jax.shard_map(
        functools.partial(on_device, mesh.shape["blk"]),
        mesh=mesh,
        in_specs=(flat, P("group"), P("group"), P("group", None)) + (deep,) * 5,
        out_specs=(deep,) * 4 + (flat,),
        check_vma=False,
    )
```

time: 69.5 us -> 45.7 us (0.66)
  Pallas kernels: 59.5 us -> 39.2 us
  local copies, waits for them, and re-layouts: 8.87 us -> 5.44 us
    pallas_call x2, Pallas kernels: 36 us -> 24.2 us  [the longest x1 21.1 us: flow(): pl.pallas_call(functools.partial(flow_kernel, n), in_specs=[hbm] * 4, out...]
    pallas_call x1, Pallas kernels: 16.3 us -> 7.67 us  [spread_tiles(): pl.pallas_call(functools.partial(spread_kernel, n, cap), out_shape=jax.Sh...]
    unnamed x20 -> x23, local copies, waits for them, and re-layouts: 8.87 us -> 5.44 us
where the time goes in v2:
time: 45.7 us; the launch traced here: 45.4 us
  Pallas kernels  39.2 us (86%)
  local copies, waits for them, and re-layouts  5.44 us (12%)
  between operations  0.75 us (2%)
    pallas_call x1, Pallas kernels, flow(): pl.pallas_call(functools.partial(flow_kernel, n), in_specs=[hbm] * 4, out...  21.1 us
    pallas_call x1, Pallas kernels, spread_tiles(): pl.pallas_call(functools.partial(spread_kernel, n, cap), out_shape=jax.Sh...  7.67 us
    pallas_call x1, Pallas kernels, solve(): pl.pallas_call(functools.partial(solve_kernel, n, cap), grid=(blocks,), i...  7.32 us
    unnamed x23, local copies, waits for them, and re-layouts  5.44 us
    pallas_call x1, Pallas kernels, scalars_mix(): pl.pallas_call(scalars_mix_kernel, grid=(blocks,), in_specs=[flat, deep,...  3.18 us

profile of v2, /device:TPU:0, one launch (start us, length us, event | category | flops | bytes accessed | tf_op | source)
XLA Modules:
  0.0 45.4 jit_solution(14126675161044069315)
XLA Ops:
  0.6 0.0 copy-start
  0.6 1.3 %copy-done = f32[4,20,32,128]{3,2,1,0:T(8,128)S(1)} copy-done((f32[4,20,32,128]{3,2,1,0:T(8,128)S(1)}, f32[4,20,32,128]{3,2,1,0:T(8,128)}, u32[]{:S(2)}) %copy-start) | copy-done | bytes 1310744
  2.0 0.0 copy-start.2
  2.0 1.3 %copy-done.2 = f32[4,20,32,128]{3,2,1,0:T(8,128)S(1)} copy-done((f32[4,20,32,128]{3,2,1,0:T(8,128)S(1)}, f32[4,20,32,128]{3,2,1,0:T(8,128)}, u32[]{:S(2)}) %copy-start.2) | copy-done | bytes 1310744
  3.3 0.0 copy-start.3
  3.3 1.3 %copy-done.3 = f32[4,20,32,128]{3,2,1,0:T(8,128)S(1)} copy-done((f32[4,20,32,128]{3,2,1,0:T(8,128)S(1)}, f32[4,20,32,128]{3,2,1,0:T(8,128)}, u32[]{:S(2)}) %copy-start.3) | copy-done | bytes 1310744
  4.6 0.0 copy-start.6
  4.6 0.8 %copy-done.6 = s32[4,32,128]{2,1,0:T(8,128)S(1)} copy-done((s32[4,32,128]{2,1,0:T(8,128)S(1)}, s32[4,32,128]{2,1,0:T(8,128)}, u32[]{:S(2)}) %copy-start.6) | copy-done | bytes 65560
  5.4 0.0 copy-start.7
  5.4 21.1 %flow.1 = (f32[4,20,32,128]{3,2,1,0:T(8,128)S(1)}, f32[4,20,32,128]{3,2,1,0:T(8,128)S(1)}, f32[4,32,128]{2,1,0:T(8,128)S(1)}, f32[4,32,128]{2,1,0:T(8,128)S(1)},...) custom-call(s32[4,32,128]{2,1,0:T(8,128)S(1)} %copy-done.6, f32[4,20,32,128]{3,2,1,0:T(8,128)S(1)} %copy-done.2, ...), custom_call_target="tpu_custom_call" | custom-call | tf_op jit(solution)/shard_map/flow/pallas_call | solution.py:302
  26.5 0.0 copy-done.7
  26.5 0.0 copy-done.8
  26.5 0.0 copy-done.9
  26.5 0.0 copy-done.10
  26.6 0.0 copy-start.1
  26.6 0.0 copy-start.4
  26.6 0.0 copy-start.5
  26.6 7.3 %solve.1 = (f32[4,20,32,128]{3,2,1,0:T(8,128)}, f32[4,20,32,128]{3,2,1,0:T(8,128)}, f32[16,2,8,128]{3,2,1,0:T(8,128)S(1)}, s32[32]{0:T(128)S(1)}) custom-call(s32[64]{0:T(128)S(1)} %copy-done.10, s32[256]{0:T(256)S(1)} %copy-done.9, s32[8,256]{1,0:T(8,128)S(1)} %bitcast.1, f32[16,4,24,128]{3,2,1,0:T(8,128)S(1)} %get-tuple-element.17.got_div, ...), custom_call_target="tpu_custom_call" | custom-call | tf_op jit(solution)/shard_map/solve/pallas_call | solution.py:577
  33.9 7.7 %spread_tiles.1 = f32[14,8,128]{2,1,0:T(8,128)S(1)} custom-call(s32[32]{0:T(128)S(1)} %get-tuple-element.27.place_ref, f32[16,2,8,128]{3,2,1,0:T(8,128)S(1)} %get-tuple-element.28.x_ref), custom_call_target="tpu_custom_call" | custom-call | tf_op jit(solution)/shard_map/spread_tiles/pallas_call | solution.py:359
  41.6 0.0 copy-done.1
  41.6 0.0 copy-done.4
  41.6 0.0 copy-done.5
  41.6 3.2 %scalars_mix.1 = (f32[4,20,32,128]{3,2,1,0:T(8,128)}, f32[4,20,32,128]{3,2,1,0:T(8,128)}) custom-call(s32[4,32,128]{2,1,0:T(8,128)S(1)} %copy-done.7, f32[4,20,32,128]{3,2,1,0:T(8,128)S(1)} %copy-done.4, f32[4,20,32,128]{3,2,1,0:T(8,128)S(1)} %copy-done.5, f32[4,20,32,128]{3,2,1,0:T(8,128)S(1)} %copy-done.1), custom_call_target="tpu_custom_call" | custom-call | tf_op jit(solution)/shard_map/scalars_mix/pallas_call | solution.py:105
  44.8 0.6 %copy.15 = f32[14,8,128]{2,1,0:T(8,128)} copy(f32[14,8,128]{2,1,0:T(8,128)S(1)} %spread_tiles.1) | data formatting | bytes 114688
  (3 shorter events, 0.0 us)
Async XLA Ops:
  0.6 1.3 %copy-start = (f32[4,20,32,128]{3,2,1,0:T(8,128)S(1)}, f32[4,20,32,128]{3,2,1,0:T(8,128)}, u32[]{:S(2)}) copy-start(f32[4,20,32,128]{3,2,1,0:T(8,128)} %k_ref.1) | copy-start | bytes 3932164
  2.0 1.3 %copy-start.2 = (f32[4,20,32,128]{3,2,1,0:T(8,128)S(1)}, f32[4,20,32,128]{3,2,1,0:T(8,128)}, u32[]{:S(2)}) copy-start(f32[4,20,32,128]{3,2,1,0:T(8,128)} %u_hbm.1) | copy-start | bytes 3932164
  3.3 1.3 %copy-start.3 = (f32[4,20,32,128]{3,2,1,0:T(8,128)S(1)}, f32[4,20,32,128]{3,2,1,0:T(8,128)}, u32[]{:S(2)}) copy-start(f32[4,20,32,128]{3,2,1,0:T(8,128)} %v_hbm.1) | copy-start | bytes 3932164
  4.6 0.8 %copy-start.6 = (s32[4,32,128]{2,1,0:T(8,128)S(1)}, s32[4,32,128]{2,1,0:T(8,128)}, u32[]{:S(2)}) copy-start(s32[4,32,128]{2,1,0:T(8,128)} %wet_ref.3) | copy-start | bytes 196612
  5.4 21.1 %copy-start.7 = (s32[4,32,128]{2,1,0:T(8,128)S(1)}, s32[4,32,128]{2,1,0:T(8,128)}, u32[]{:S(2)}) copy-start(s32[4,32,128]{2,1,0:T(8,128)} %wet_ref.3) | copy-start | bytes 196612
  5.4 21.1 %copy-start.8 = (s32[256,8]{0,1:T(8,128)S(1)}, s32[256,8]{0,1:T(8,128)}, u32[]{:S(2)}) copy-start(s32[256,8]{0,1:T(8,128)} %param.12) | copy-start | bytes 24580
  5.4 21.1 %copy-start.9 = (s32[256]{0:T(256)S(1)}, s32[256]{0:T(256)}, u32[]{:S(2)}) copy-start(s32[256]{0:T(256)} %owner_ref.1) | copy-start | bytes 3076
  5.4 21.1 %copy-start.10 = (s32[64]{0:T(128)S(1)}, s32[64]{0:T(128)}, u32[]{:S(2)}) copy-start(s32[64]{0:T(128)} %runs_ref.1) | copy-start | bytes 772
  26.6 15.0 %copy-start.1 = (f32[4,20,32,128]{3,2,1,0:T(8,128)S(1)}, f32[4,20,32,128]{3,2,1,0:T(8,128)}, u32[]{:S(2)}) copy-start(f32[4,20,32,128]{3,2,1,0:T(8,128)} %k_ref.1) | copy-start | bytes 3932164
  26.6 15.0 %copy-start.4 = (f32[4,20,32,128]{3,2,1,0:T(8,128)S(1)}, f32[4,20,32,128]{3,2,1,0:T(8,128)}, u32[]{:S(2)}) copy-start(f32[4,20,32,128]{3,2,1,0:T(8,128)} %t_ref.1) | copy-start | bytes 3932164
  26.6 15.0 %copy-start.5 = (f32[4,20,32,128]{3,2,1,0:T(8,128)S(1)}, f32[4,20,32,128]{3,2,1,0:T(8,128)}, u32[]{:S(2)}) copy-start(f32[4,20,32,128]{3,2,1,0:T(8,128)} %s_ref.1) | copy-start | bytes 3932164

commit v3 on v2

--- a/solution.py
+++ b/solution.py
@@ -19,6 +19,7 @@
 STRIP = 16
 PACK = 24
 TALL = 48
+FLOW_VMEM = 47 * 2**20
 
 damping = 0.1
 coriolis = 0.3
@@ -64,56 +65,6 @@
     return out
 
 
-def scalars_mix_kernel(wet_ref, t_ref, s_ref, k_ref, tm_ref, sm_ref, half_ref):
-    def strip(index, carry):
-        rows = pl.ds(pl.multiple_of(index * STRIP, STRIP), STRIP)
-        wet = wet_ref[rows, :]
-        zero = jnp.zeros((STRIP, COLS), jnp.float32)
-        lower = ratio = tv = sv = zero
-        for k in range(LEVELS):
-            step = STEPS[k]
-            if k + 1 < LEVELS:
-                upper = jnp.where(wet > k + 1, 0.5 * k_ref[k, rows, :], 0.0)
-            else:
-                upper = zero
-            inv = 1.0 / (step + upper + lower * (1.0 - ratio))
-            tv = (step * t_ref[k, rows, :] + lower * tv) * inv
-            sv = (step * s_ref[k, rows, :] + lower * sv) * inv
-            ratio = upper * inv
-            tm_ref[k, rows, :] = tv
-            sm_ref[k, rows, :] = sv
-            half_ref[k] = ratio
-            lower = upper
-        last = LEVELS - 1
-        tm_ref[last, rows, :] = jnp.where(wet > last, tv, 0.0)
-        sm_ref[last, rows, :] = jnp.where(wet > last, sv, 0.0)
-        for k in range(last - 1, -1, -1):
-            ratio = half_ref[k]
-            tv = tm_ref[k, rows, :] + ratio * tv
-            sv = sm_ref[k, rows, :] + ratio * sv
-            tm_ref[k, rows, :] = jnp.where(wet > k, tv, 0.0)
-            sm_ref[k, rows, :] = jnp.where(wet > k, sv, 0.0)
-        return carry
-
-    lax.fori_loop(0, ROWS // STRIP, strip, 0)
-
-
-def scalars_mix(wet, t, s, kappa):
-    blocks = t.shape[0]
-    deep = pl.BlockSpec((None, LEVELS, ROWS, COLS), lambda i: (i, 0, 0, 0))
-    flat = pl.BlockSpec((None, ROWS, COLS), lambda i: (i, 0, 0))
-    return pl.pallas_call(
-        scalars_mix_kernel,
-        grid=(blocks,),
-        in_specs=[flat, deep, deep, deep],
-        out_specs=[deep, deep],
-        out_shape=[jax.ShapeDtypeStruct(t.shape, jnp.float32)] * 2,
-        scratch_shapes=[pltpu.VMEM((LEVELS, STRIP, COLS), jnp.float32)],
-        compiler_params=pltpu.CompilerParams(vmem_limit_bytes=24 * 2**20),
-        name="scalars_mix",
-    )(wet, t, s, kappa)
-
-
 def greet(n, me):
     barrier = pltpu.get_barrier_semaphore()
 
@@ -190,10 +141,11 @@
 
 
 def flow_kernel(
-    n, wet_hbm, u_hbm, v_hbm, k_hbm,
-    um_ref, vm_ref, div_ref, depth_ref, got_div, got_depth,
-    wet_ref, u_ref, v_ref, k_ref, ratio_ref, zonal_ref, north_ref, div_pack, depth_pack,
-    wet_sem, u_sem, v_sem, k_sem, div_send, div_recv, depth_send, depth_recv,
+    n, wet_hbm, u_hbm, v_hbm, k_hbm, t_hbm, s_hbm,
+    um_ref, vm_ref, tm_ref, sm_ref, div_ref, depth_ref, got_div, got_depth,
+    wet_ref, u_ref, v_ref, k_ref, t_ref, s_ref,
+    ratio_ref, zonal_ref, north_ref, div_pack, depth_pack,
+    wet_sem, u_sem, v_sem, k_sem, t_sem, s_sem, div_send, div_recv, depth_send, depth_recv,
 ):
     me = lax.axis_index("blk")
     relay_depth = Relay(n, me, depth_pack, got_depth, depth_send, depth_recv)
@@ -204,15 +156,19 @@
     wet_copy = pltpu.make_async_copy(wet_hbm, wet_ref, wet_sem)
     wet_copy.start()
 
-    def fetch(block):
+    flows = ((k_hbm, k_ref, k_sem), (u_hbm, u_ref, u_sem), (v_hbm, v_ref, v_sem))
+    tracers = ((t_hbm, t_ref, t_sem), (s_hbm, s_ref, s_sem))
+
+    def fetch(what, block):
         return [
             pltpu.make_async_copy(hbm.at[block], ref.at[block], sem.at[block])
-            for hbm, ref, sem in ((u_hbm, u_ref, u_sem), (v_hbm, v_ref, v_sem), (k_hbm, k_ref, k_sem))
+            for hbm, ref, sem in what
         ]
 
-    for block in range(BLK_DEV):
-        for copy in fetch(block):
-            copy.start()
+    for what in (flows, tracers):
+        for block in range(BLK_DEV):
+            for copy in fetch(what, block):
+                copy.start()
     wet_copy.wait()
     for block in range(BLK_DEV):
         count = wet_ref[block].astype(jnp.float32)
@@ -225,7 +181,7 @@
     relay_depth.start()
 
     def one_block(block, carry):
-        for copy in fetch(block):
+        for copy in fetch(flows, block):
             copy.wait()
 
         def strip(index, inner):
@@ -281,17 +237,53 @@
         div_pack[block, 16:24] = side_pack(div, zonal)
         return carry
 
-    lax.fori_loop(0, BLK_DEV, one_block, 0)
+    def one_tracer(block, carry):
+        for copy in fetch(tracers, block):
+            copy.wait()
+
+        def strip(index, inner):
+            rows = pl.ds(pl.multiple_of(index * STRIP, STRIP), STRIP)
+            wet = wet_ref[block, rows, :]
+            zero = jnp.zeros((STRIP, COLS), jnp.float32)
+            lower = ratio = tv = sv = zero
+            for k in range(LEVELS):
+                step = STEPS[k]
+                if k + 1 < LEVELS:
+                    upper = jnp.where(wet > k + 1, 0.5 * k_ref[block, k, rows, :], 0.0)
+                else:
+                    upper = zero
+                inv = 1.0 / (step + upper + lower * (1.0 - ratio))
+                tv = (step * t_ref[block, k, rows, :] + lower * tv) * inv
+                sv = (step * s_ref[block, k, rows, :] + lower * sv) * inv
+                ratio = upper * inv
+                tm_ref[block, k, rows, :] = tv
+                sm_ref[block, k, rows, :] = sv
+                ratio_ref[k] = ratio
+                lower = upper
+            for k in range(LEVELS - 2, -1, -1):
+                ratio = ratio_ref[k]
+                tv = tm_ref[block, k, rows, :] + ratio * tv
+                sv = sm_ref[block, k, rows, :] + ratio * sv
+                tm_ref[block, k, rows, :] = tv
+                sm_ref[block, k, rows, :] = sv
+            return inner
+
+        lax.fori_loop(0, ROWS // STRIP, strip, 0)
+        return carry
+
+    lax.fori_loop(0, 3, one_block, 0)
+    relay_depth.second()
+    lax.fori_loop(3, BLK_DEV, one_block, 0)
     relay_div.start()
-    relay_depth.second()
     relay_depth.third()
+    lax.fori_loop(0, BLK_DEV, one_tracer, 0)
     relay_div.second()
     relay_div.third()
     relay_depth.finish()
     relay_div.finish()
 
 
-def flow(n, wet, u, v, kappa):
+def flow(n, wet, u, v, kappa, t, s):
     blocks = u.shape[0]
     deep = jax.ShapeDtypeStruct(u.shape, jnp.float32)
     flat = jax.ShapeDtypeStruct((blocks, ROWS, COLS), jnp.float32)
@@ -301,14 +293,12 @@
     pack = pltpu.VMEM((blocks, PACK, COLS), jnp.float32)
     return pl.pallas_call(
         functools.partial(flow_kernel, n),
-        in_specs=[hbm] * 4,
-        out_specs=[vmem] * 6,
-        out_shape=[deep, deep, flat, flat, got, got],
-        scratch_shapes=[
-            pltpu.VMEM(wet.shape, jnp.int32),
-            pltpu.VMEM(u.shape, jnp.float32),
-            pltpu.VMEM(u.shape, jnp.float32),
-            pltpu.VMEM(u.shape, jnp.float32),
+        in_specs=[hbm] * 6,
+        out_specs=[vmem] * 8,
+        out_shape=[deep, deep, deep, deep, flat, flat, got, got],
+        scratch_shapes=[pltpu.VMEM(wet.shape, jnp.int32)]
+        + [pltpu.VMEM(u.shape, jnp.float32)] * 5
+        + [
             pltpu.VMEM((LEVELS, STRIP, COLS), jnp.float32),
             pltpu.VMEM((ROWS, COLS), jnp.float32),
             pltpu.VMEM((ROWS, COLS), jnp.float32),
@@ -316,13 +306,13 @@
             pack,
             pltpu.SemaphoreType.DMA,
         ]
-        + [pltpu.SemaphoreType.DMA((blocks,))] * 3
+        + [pltpu.SemaphoreType.DMA((blocks,))] * 5
         + [pltpu.SemaphoreType.DMA((n,))] * 4,
         compiler_params=pltpu.CompilerParams(
-            collective_id=0, has_side_effects=True, vmem_limit_bytes=28 * 2**20
+            collective_id=0, has_side_effects=True, vmem_limit_bytes=FLOW_VMEM
         ),
         name="flow",
-    )(wet, u, v, kappa)
+    )(wet, u, v, kappa, t, s)
 
 
 def spread_kernel(n, cap, place_ref, x_ref, out_ref, held, send_sem, recv_sem):
@@ -404,8 +394,9 @@
 
 
 def solve_kernel(
-    n, cap, runs_ref, owner_ref, near, got_div, got_depth, div_ref, depth_ref, wet_ref, um_ref, vm_ref,
-    un_ref, vn_ref, out_ref, place_ref,
+    n, cap, runs_ref, owner_ref, near, got_div, got_depth, div_ref, depth_ref, wet_ref,
+    um_ref, vm_ref, tm_ref, sm_ref,
+    un_ref, vn_ref, tn_ref, sn_ref, out_ref, place_ref,
     scalars, counts,
 ):
     step = pl.program_id(0)
@@ -564,57 +555,44 @@
     wet = wet_ref[...]
     for k in range(LEVELS):
         wetted = wet > k
-        un_ref[k] = jnp.where(wetted, um_ref[k] - east, 0.0)
-        vn_ref[k] = jnp.where(wetted, vm_ref[k] - south, 0.0)
-
-
-def solve(n, cap, patch_owner, piece_owner, near, got_div, got_depth, div, depth, wet, um, vm):
-    blocks = um.shape[0]
+        un_ref[k] = jnp.where(wetted, um_ref[step, k] - east, 0.0)
+        vn_ref[k] = jnp.where(wetted, vm_ref[step, k] - south, 0.0)
+        tn_ref[k] = jnp.where(wetted, tm_ref[step, k], 0.0)
+        sn_ref[k] = jnp.where(wetted, sm_ref[step, k], 0.0)
+
+
+def solve(n, cap, patch_owner, piece_owner, near, got_div, got_depth, div, depth, wet, fields):
+    blocks = wet.shape[0]
     deep = pl.BlockSpec((None, LEVELS, ROWS, COLS), lambda i: (i, 0, 0, 0))
     flat = pl.BlockSpec((None, ROWS, COLS), lambda i: (i, 0, 0))
-    deep_shape = jax.ShapeDtypeStruct(um.shape, jnp.float32)
+    deep_shape = jax.ShapeDtypeStruct(fields[0].shape, jnp.float32)
     smem = pl.BlockSpec(memory_space=pltpu.SMEM)
+    vmem = pl.BlockSpec(memory_space=pltpu.VMEM)
     return pl.pallas_call(
         functools.partial(solve_kernel, n, cap),
         grid=(blocks,),
-        in_specs=[
-            smem,
-            smem,
-            smem,
-            pl.BlockSpec(memory_space=pltpu.VMEM),
-            pl.BlockSpec(memory_space=pltpu.VMEM),
-            flat,
-            flat,
-            flat,
-            deep,
-            deep,
-        ],
-        out_specs=[deep, deep, pl.BlockSpec((n, cap, TY, COLS), lambda i: (0, 0, 0, 0)), smem],
-        out_shape=[
-            deep_shape,
-            deep_shape,
+        in_specs=[smem] * 3 + [vmem] * 2 + [flat] * 3 + [vmem] * 4,
+        out_specs=[deep] * 4 + [pl.BlockSpec((n, cap, TY, COLS), lambda i: (0, 0, 0, 0)), smem],
+        out_shape=[deep_shape] * 4
+        + [
             jax.ShapeDtypeStruct((n, cap, TY, COLS), jnp.float32),
             jax.ShapeDtypeStruct((2 * BT_DEV + 4,), jnp.int32),
         ],
-        scratch_shapes=[
-            pltpu.SMEM((1,), jnp.int32),
-            pltpu.SMEM((n,), jnp.int32),
-        ],
-        compiler_params=pltpu.CompilerParams(vmem_limit_bytes=48 * 2**20),
+        scratch_shapes=[pltpu.SMEM((1,), jnp.int32), pltpu.SMEM((n,), jnp.int32)],
+        compiler_params=pltpu.CompilerParams(vmem_limit_bytes=40 * 2**20),
         name="solve",
-    )(patch_owner, piece_owner, near, got_div, got_depth, div, depth, wet, um, vm)
+    )(patch_owner, piece_owner, near, got_div, got_depth, div, depth, wet, *fields)
 
 
 def on_device(n, wet, patch_owner, piece_owner, neighbours, u, v, t, s, kappa):
     cap = max(2, TILES_DEV // n)
-    um, vm, div, depth, got_div, got_depth = flow(n, wet, u, v, kappa)
-    tm, sm = scalars_mix(wet, t, s, kappa)
-    un, vn, tiles, place = solve(
+    um, vm, tm, sm, div, depth, got_div, got_depth = flow(n, wet, u, v, kappa, t, s)
+    un, vn, tn, sn, tiles, place = solve(
         n, cap, patch_owner, piece_owner, neighbours.T,
-        got_div, got_depth, div, depth, wet, um, vm,
+        got_div, got_depth, div, depth, wet, (um, vm, tm, sm),
     )
     height = spread_tiles(n, cap, place, tiles)
-    return (un, vn, tm, sm, height)
+    return (un, vn, tn, sn, height)
 
 
 def solution(mesh):

time: 45.7 us -> 39.2 us (0.86)
  local copies, waits for them, and re-layouts: 5.44 us -> 1.47 us
  Pallas kernels: 39.2 us -> 36.9 us
    unnamed x23 -> x9, local copies, waits for them, and re-layouts: 5.44 us -> 1.47 us
    pallas_call x2 -> x1, Pallas kernels: 24.2 us -> 21.1 us  [flow(): pl.pallas_call(functools.partial(flow_kernel, n), in_specs=[hbm] * 6, out...]
    pallas_call x1, Pallas kernels: 7.32 us -> 7.84 us  [solve(): pl.pallas_call(functools.partial(solve_kernel, n, cap), grid=(blocks,), i...]
where the time goes in v3:
time: 39.2 us; the launch traced here: 39 us
  Pallas kernels  36.9 us (94%)
  local copies, waits for them, and re-layouts  1.47 us (4%)
  between operations  0.68 us (2%)
    pallas_call x1, Pallas kernels, flow(): pl.pallas_call(functools.partial(flow_kernel, n), in_specs=[hbm] * 6, out...  21.1 us
    pallas_call x1, Pallas kernels, spread_tiles(): pl.pallas_call(functools.partial(spread_kernel, n, cap), out_shape=jax.Sh...  7.88 us
    pallas_call x1, Pallas kernels, solve(): pl.pallas_call(functools.partial(solve_kernel, n, cap), grid=(blocks,), i...  7.84 us
    unnamed x9, local copies, waits for them, and re-layouts  1.47 us

profile of v3, /device:TPU:0, one launch (start us, length us, event | category | flops | bytes accessed | tf_op | source)
XLA Modules:
  0.0 39.0 jit_solution(9707901596175163916)
XLA Ops:
  0.6 0.0 copy-start
  0.6 0.8 %copy-done = s32[4,32,128]{2,1,0:T(8,128)S(1)} copy-done((s32[4,32,128]{2,1,0:T(8,128)S(1)}, s32[4,32,128]{2,1,0:T(8,128)}, u32[]{:S(2)}) %copy-start) | copy-done | bytes 65560
  1.5 0.0 copy-start.1
  1.5 0.0 copy-start.2
  1.5 0.0 copy-start.3
  1.5 21.1 %flow.1 = (f32[4,20,32,128]{3,2,1,0:T(8,128)S(1)}, f32[4,20,32,128]{3,2,1,0:T(8,128)S(1)}, f32[4,20,32,128]{3,2,1,0:T(8,128)S(1)}, f32[4,20,32,128]{3,2,1,0:T(8,...) custom-call(s32[4,32,128]{2,1,0:T(8,128)S(1)} %copy-done, ...), custom_call_target="tpu_custom_call" | custom-call | tf_op jit(solution)/shard_map/flow/pallas_call | solution.py:294
  22.6 0.0 copy-done.1
  22.6 0.0 copy-done.2
  22.7 0.0 copy-done.3
  22.7 7.8 %solve.1 = (f32[4,20,32,128]{3,2,1,0:T(8,128)}, f32[4,20,32,128]{3,2,1,0:T(8,128)}, f32[4,20,32,128]{3,2,1,0:T(8,128)}, f32[4,20,32,128]{3,2,1,0:T(8,128)}, f32[...) custom-call(s32[64]{0:T(128)S(1)} %copy-done.3, s32[256]{0:T(256)S(1)} %copy-done.2, s32[8,256]{1,0:T(8,128)S(1)} %bitcast.1, ...), custom_call_target="tpu_custom_call" | custom-call | tf_op jit(solution)/shard_map/solve/pallas_call | solution.py:571
  30.5 7.9 %spread_tiles.1 = f32[14,8,128]{2,1,0:T(8,128)S(1)} custom-call(s32[32]{0:T(128)S(1)} %get-tuple-element.31.place_ref, f32[16,2,8,128]{3,2,1,0:T(8,128)S(1)} %get-tuple-element.32.x_ref), custom_call_target="tpu_custom_call" | custom-call | tf_op jit(solution)/shard_map/spread_tiles/pallas_call | solution.py:349
  38.4 0.6 %copy.15 = f32[14,8,128]{2,1,0:T(8,128)} copy(f32[14,8,128]{2,1,0:T(8,128)S(1)} %spread_tiles.1) | data formatting | bytes 114688
Async XLA Ops:
  0.6 0.8 %copy-start = (s32[4,32,128]{2,1,0:T(8,128)S(1)}, s32[4,32,128]{2,1,0:T(8,128)}, u32[]{:S(2)}) copy-start(s32[4,32,128]{2,1,0:T(8,128)} %wet_ref.1) | copy-start | bytes 196612
  1.5 21.2 %copy-start.1 = (s32[256,8]{0,1:T(8,128)S(1)}, s32[256,8]{0,1:T(8,128)}, u32[]{:S(2)}) copy-start(s32[256,8]{0,1:T(8,128)} %param.12) | copy-start | bytes 24580
  1.5 21.2 %copy-start.2 = (s32[256]{0:T(256)S(1)}, s32[256]{0:T(256)}, u32[]{:S(2)}) copy-start(s32[256]{0:T(256)} %owner_ref.1) | copy-start | bytes 3076
  1.5 21.2 %copy-start.3 = (s32[64]{0:T(128)S(1)}, s32[64]{0:T(128)}, u32[]{:S(2)}) copy-start(s32[64]{0:T(128)} %runs_ref.1) | copy-start | bytes 772

commit v4 on v3

--- a/solution.py
+++ b/solution.py
@@ -19,7 +19,7 @@
 STRIP = 16
 PACK = 24
 TALL = 48
-FLOW_VMEM = 47 * 2**20
+FLOW_VMEM = 95 * 2**19
 
 damping = 0.1
 coriolis = 0.3
@@ -52,16 +52,17 @@
     return lax.broadcasted_iota(jnp.int32, shape, 0)
 
 
-def side_pack(field, edge):
+def side_pack(div, depth, edge):
     lane = lane_of((TY, COLS))
     out = jnp.zeros((TY, COLS), jnp.float32)
     for group in range(SUB):
-        rows = field[group * TY : (group + 1) * TY]
-        moved = pltpu.roll(rows, (16 + 32 * group) % COLS, 1)
-        out = jnp.where(lane // 32 == group, moved, out)
-        if edge is not None:
-            moved = pltpu.roll(edge[group * TY : (group + 1) * TY], (1 + 32 * group) % COLS, 1)
-            out = jnp.where(lane == 32 * group, moved, out)
+        rows = slice(group * TY, (group + 1) * TY)
+        moved = pltpu.roll(div[rows], 8 + 32 * group, 1)
+        out = jnp.where(lane // 16 == 2 * group, moved, out)
+        moved = pltpu.roll(depth[rows], (24 + 32 * group) % COLS, 1)
+        out = jnp.where(lane // 16 == 2 * group + 1, moved, out)
+        moved = pltpu.roll(edge[rows], 1 + 32 * group, 1)
+        out = jnp.where(lane == 32 * group, moved, out)
     return out
 
 
@@ -176,7 +177,6 @@
         depth_ref[block] = depth
         depth_pack[block, 0:8] = depth[0:8]
         depth_pack[block, 8:16] = depth[24:32]
-        depth_pack[block, 16:24] = side_pack(depth, None)
     pl.semaphore_wait(barrier, len(relay_depth.peers))
     relay_depth.start()
 
@@ -234,7 +234,7 @@
         div_pack[block, 8:16] = jnp.where(
             row_of((TY, COLS)) == 0, pltpu.roll(north[24:32], 1, 0), div[24:32]
         )
-        div_pack[block, 16:24] = side_pack(div, zonal)
+        div_pack[block, 16:24] = side_pack(div, depth_ref[block], zonal)
         return carry
 
     def one_tracer(block, carry):
@@ -271,13 +271,12 @@
         lax.fori_loop(0, ROWS // STRIP, strip, 0)
         return carry
 
-    lax.fori_loop(0, 3, one_block, 0)
+    lax.fori_loop(0, BLK_DEV, one_block, 0)
+    relay_div.start()
     relay_depth.second()
-    lax.fori_loop(3, BLK_DEV, one_block, 0)
-    relay_div.start()
-    relay_depth.third()
     lax.fori_loop(0, BLK_DEV, one_tracer, 0)
     relay_div.second()
+    relay_depth.third()
     relay_div.third()
     relay_depth.finish()
     relay_div.finish()
@@ -287,23 +286,23 @@
     blocks = u.shape[0]
     deep = jax.ShapeDtypeStruct(u.shape, jnp.float32)
     flat = jax.ShapeDtypeStruct((blocks, ROWS, COLS), jnp.float32)
-    got = jax.ShapeDtypeStruct((n, blocks, PACK, COLS), jnp.float32)
+    got_div = jax.ShapeDtypeStruct((n, blocks, PACK, COLS), jnp.float32)
+    got_depth = jax.ShapeDtypeStruct((n, blocks, 2 * TY, COLS), jnp.float32)
     vmem = pl.BlockSpec(memory_space=pltpu.VMEM)
     hbm = pl.BlockSpec(memory_space=pltpu.MemorySpace.HBM)
-    pack = pltpu.VMEM((blocks, PACK, COLS), jnp.float32)
     return pl.pallas_call(
         functools.partial(flow_kernel, n),
         in_specs=[hbm] * 6,
         out_specs=[vmem] * 8,
-        out_shape=[deep, deep, deep, deep, flat, flat, got, got],
+        out_shape=[deep, deep, deep, deep, flat, flat, got_div, got_depth],
         scratch_shapes=[pltpu.VMEM(wet.shape, jnp.int32)]
         + [pltpu.VMEM(u.shape, jnp.float32)] * 5
         + [
             pltpu.VMEM((LEVELS, STRIP, COLS), jnp.float32),
             pltpu.VMEM((ROWS, COLS), jnp.float32),
             pltpu.VMEM((ROWS, COLS), jnp.float32),
-            pack,
-            pack,
+            pltpu.VMEM((blocks, PACK, COLS), jnp.float32),
+            pltpu.VMEM((blocks, 2 * TY, COLS), jnp.float32),
             pltpu.SemaphoreType.DMA,
         ]
         + [pltpu.SemaphoreType.DMA((blocks,))] * 5
@@ -415,19 +414,21 @@
 
         lax.fori_loop(0, n, clear, 0)
 
-        def scan(j, place):
-            source = runs_ref[j * BLK_DEV]
-            rank = 0
-            for a in range(TILES_DEV):
-                hit = (owner_ref[j * TILES_DEV + a] == me).astype(jnp.int32)
-                place_ref[2 * place] = source
-                place_ref[2 * place + 1] = rank
-                place = place + hit
-                rank = jnp.minimum(rank + hit, cap - 1)
-            return place
-
-        lax.fori_loop(0, n, scan, 0)
-
+        scalars[1] = 0
+
+    place = scalars[1]
+    share = n // BLK_DEV
+    for part in range(share):
+        j = step * share + part
+        source = runs_ref[j * BLK_DEV]
+        rank = 0
+        for a in range(TILES_DEV):
+            hit = (owner_ref[j * TILES_DEV + a] == me).astype(jnp.int32)
+            place_ref[2 * place] = source
+            place_ref[2 * place + 1] = rank
+            place = place + hit
+            rank = jnp.minimum(rank + hit, cap - 1)
+    scalars[1] = place
     run = scalars[0]
     base = step * SUB
 
@@ -465,11 +466,13 @@
         mixed = jnp.where(lane8 < TY, load(got, who_right, start), load(got, who_left, start))
         return jnp.where((lane8 < TY) | (lane8 >= COLS - TY), mixed, 0.0)
 
-    def beside(got):
-        packed = jnp.where(lane8 % 32 >= 16, load(got, right, 16), load(got, left, 16))
+    def beside(offset):
+        packed = jnp.where(
+            lane8 % 32 >= offset, load(got_div, right, 16), load(got_div, left, 16)
+        )
         parts = []
         for group in range(SUB):
-            moved = pltpu.roll(packed, (112 - 32 * group) % COLS, 1)
+            moved = pltpu.roll(packed, (COLS - offset - 32 * group) % COLS, 1)
             parts.append(jnp.where((lane8 < TY) | (lane8 >= COLS - TY), moved, 0.0))
         return parts
 
@@ -488,7 +491,7 @@
     )
     depth_side = jnp.concatenate(
         [corner(got_depth, above_left, above_right, 8)]
-        + beside(got_depth)
+        + beside(24)
         + [corner(got_depth, below_left, below_right, 0)],
         axis=0,
     )
@@ -496,7 +499,7 @@
     top_side = corner(got_div, above_left, above_right, 8)
     first_row = row8 == 0
     mid_main = div_ref[...]
-    mid_side = beside(got_div)
+    mid_side = beside(8)
     own_main = mid_main[0:8] - jnp.where(first_row, top_main, 0.0)
     mid_side[0] = mid_side[0] - jnp.where(first_row, top_side, 0.0)
     low_main = load(got_div, below, 0) - jnp.where(first_row, load(got_div, own, 8), 0.0)
@@ -578,7 +581,7 @@
             jax.ShapeDtypeStruct((n, cap, TY, COLS), jnp.float32),
             jax.ShapeDtypeStruct((2 * BT_DEV + 4,), jnp.int32),
         ],
-        scratch_shapes=[pltpu.SMEM((1,), jnp.int32), pltpu.SMEM((n,), jnp.int32)],
+        scratch_shapes=[pltpu.SMEM((2,), jnp.int32), pltpu.SMEM((n,), jnp.int32)],
         compiler_params=pltpu.CompilerParams(vmem_limit_bytes=40 * 2**20),
         name="solve",
     )(patch_owner, piece_owner, near, got_div, got_depth, div, depth, wet, *fields)

time: 39.2 us -> 36.5 us (0.931)
  Pallas kernels: 36.9 us -> 34.1 us
    pallas_call x1, Pallas kernels: 21.1 us -> 18.3 us  [flow(): pl.pallas_call(functools.partial(flow_kernel, n), in_specs=[hbm] * 6, out...]
    pallas_call x1, Pallas kernels: 7.88 us -> 8.31 us  [spread_tiles(): pl.pallas_call(functools.partial(spread_kernel, n, cap), out_shape=jax.Sh...]
where the time goes in v4:
time: 36.5 us; the launch traced here: 36.3 us
  Pallas kernels  34.1 us (93%)
  local copies, waits for them, and re-layouts  1.47 us (4%)
  between operations  0.68 us (2%)
    pallas_call x1, Pallas kernels, flow(): pl.pallas_call(functools.partial(flow_kernel, n), in_specs=[hbm] * 6, out...  18.3 us
    pallas_call x1, Pallas kernels, spread_tiles(): pl.pallas_call(functools.partial(spread_kernel, n, cap), out_shape=jax.Sh...  8.31 us
    pallas_call x1, Pallas kernels, solve(): pl.pallas_call(functools.partial(solve_kernel, n, cap), grid=(blocks,), i...  7.55 us
    unnamed x9, local copies, waits for them, and re-layouts  1.47 us

profile of v4, /device:TPU:0, one launch (start us, length us, event | category | flops | bytes accessed | tf_op | source)
XLA Modules:
  0.0 36.3 jit_solution(4191322054031024219)
XLA Ops:
  0.6 0.0 copy-start
  0.6 0.8 %copy-done = s32[4,32,128]{2,1,0:T(8,128)S(1)} copy-done((s32[4,32,128]{2,1,0:T(8,128)S(1)}, s32[4,32,128]{2,1,0:T(8,128)}, u32[]{:S(2)}) %copy-start) | copy-done | bytes 65560
  1.5 0.0 copy-start.1
  1.5 0.0 copy-start.2
  1.5 0.0 copy-start.3
  1.5 18.3 %flow.1 = (f32[4,20,32,128]{3,2,1,0:T(8,128)S(1)}, f32[4,20,32,128]{3,2,1,0:T(8,128)S(1)}, f32[4,20,32,128]{3,2,1,0:T(8,128)S(1)}, f32[4,20,32,128]{3,2,1,0:T(8,...) custom-call(s32[4,32,128]{2,1,0:T(8,128)S(1)} %copy-done, ...), custom_call_target="tpu_custom_call" | custom-call | tf_op jit(solution)/shard_map/flow/pallas_call | solution.py:293
  19.8 0.0 copy-done.1
  19.8 0.0 copy-done.2
  19.8 0.0 copy-done.3
  19.8 7.5 %solve.1 = (f32[4,20,32,128]{3,2,1,0:T(8,128)}, f32[4,20,32,128]{3,2,1,0:T(8,128)}, f32[4,20,32,128]{3,2,1,0:T(8,128)}, f32[4,20,32,128]{3,2,1,0:T(8,128)}, f32[...) custom-call(s32[64]{0:T(128)S(1)} %copy-done.3, s32[256]{0:T(256)S(1)} %copy-done.2, s32[8,256]{1,0:T(8,128)S(1)} %bitcast.1, ...), custom_call_target="tpu_custom_call" | custom-call | tf_op jit(solution)/shard_map/solve/pallas_call | solution.py:574
  27.4 8.3 %spread_tiles.1 = f32[14,8,128]{2,1,0:T(8,128)S(1)} custom-call(s32[32]{0:T(128)S(1)} %get-tuple-element.31.place_ref, f32[16,2,8,128]{3,2,1,0:T(8,128)S(1)} %get-tuple-element.32.x_ref), custom_call_target="tpu_custom_call" | custom-call | tf_op jit(solution)/shard_map/spread_tiles/pallas_call | solution.py:348
  35.7 0.6 %copy.15 = f32[14,8,128]{2,1,0:T(8,128)} copy(f32[14,8,128]{2,1,0:T(8,128)S(1)} %spread_tiles.1) | data formatting | bytes 114688
Async XLA Ops:
  0.6 0.8 %copy-start = (s32[4,32,128]{2,1,0:T(8,128)S(1)}, s32[4,32,128]{2,1,0:T(8,128)}, u32[]{:S(2)}) copy-start(s32[4,32,128]{2,1,0:T(8,128)} %wet_ref.1) | copy-start | bytes 196612
  1.5 18.3 %copy-start.1 = (s32[256,8]{0,1:T(8,128)S(1)}, s32[256,8]{0,1:T(8,128)}, u32[]{:S(2)}) copy-start(s32[256,8]{0,1:T(8,128)} %param.12) | copy-start | bytes 24580
  1.5 18.3 %copy-start.2 = (s32[256]{0:T(256)S(1)}, s32[256]{0:T(256)}, u32[]{:S(2)}) copy-start(s32[256]{0:T(256)} %owner_ref.1) | copy-start | bytes 3076
  1.5 18.3 %copy-start.3 = (s32[64]{0:T(128)S(1)}, s32[64]{0:T(128)}, u32[]{:S(2)}) copy-start(s32[64]{0:T(128)} %runs_ref.1) | copy-start | bytes 772
